TPU v7x, 512 devices: a whole 4x4x16 slice. The times are simulated.
512 devices in a mesh: cfd: 64 (over y, z), obs: 8 (over x, core).
Axes of the slice: x: 4, y: 4, z: 16, core: 2. Of those that a mesh axis runs over, the one named last changes fastest.
Arguments:
- flow_field: float32 [4, 1024, 128, 128], P(None, 'cfd', 'obs'), may hold values from -6 to 6
- disk_mask: int32 [1024, 128, 128], P('cfd', 'obs'), may hold values 0 or 1
- surf_cell: int32 [8, 8192], P('obs', 'cfd'), may hold values from 0 to 32767
- delay_bin: int32 [8, 8192], P('obs', 'cfd'), may hold values from 0 to 505
- tap_phase: int32 [8, 8192], P('obs', 'cfd'), may hold values from 0 to 3
- panel_counts: int32 [8, 64], replicated, may hold values from 1 to 128, 4096 in all within a row
- observer_pos: float32 [3, 8192], P(None, 'cfd'), may hold values from 0 to 1
Outputs:
- flow_out: float32 [4, 1024, 128, 128], P(None, 'cfd', 'obs')
- pressure_signal: float32 [8192, 512], P(('cfd', 'obs'))
Inputs may be any that keep to these rules, and one draw needn't show every extreme that they name: `panel_counts`: every row sums to 4096, and every row has an entry equal to 128.
All inputs are finite; a program needn't handle non-finite values. No bound on the sum of `disk_mask` on one device may be relied on, other than what follows from the above.
Results may differ from a plain program's by a relative error of at most 0.0041.
Values sent between devices are 32-bit elements; how exact they have to be, the bound alone decides.
A program may use at most 128 MiB of HBM per device.

v0:
```python
import jax
import jax.numpy as jnp
from jax import lax
from jax.sharding import PartitionSpec as P

STEPS = 4
SAMPLES = 512


def extended(array, sides, width):
    for axis, dim in sides:
        size, length = (lax.axis_size(axis), array.shape[dim])
        up = [(i, (i + 1) % size) for i in range(size - 1)]
        down = [(j, i) for i, j in up]
        last = lax.slice_in_dim(array, length - width, length, axis=dim)
        first = lax.slice_in_dim(array, 0, width, axis=dim)
        before = lax.ppermute(last, axis, up)
        after = lax.ppermute(first, axis, down)
        array = jnp.concatenate([before, array, after], axis=dim)
    return array


def advance(state, padded, mask_float):
    x_plus = padded[:, 2:, 1:-1, 1:-1]
    x_minus = padded[:, :-2, 1:-1, 1:-1]
    y_plus = padded[:, 1:-1, 2:, 1:-1]
    y_minus = padded[:, 1:-1, :-2, 1:-1]
    z_plus = padded[:, 1:-1, 1:-1, 2:]
    z_minus = padded[:, 1:-1, 1:-1, :-2]
    laplace = x_plus + x_minus + y_plus + y_minus + z_plus + z_minus - 6.0 * state
    moved = state + 0.1 * laplace + 0.3 * (x_minus - state)
    pressure = moved[0] + 0.5 * mask_float * state[1]
    velocity = moved[1:] - 0.4 * mask_float[None] * state[1:]
    return jnp.concatenate([pressure[None], velocity], axis=0)


def lagrange(phase):
    frac = phase * 0.25
    return [
        -frac * (frac - 1.0) * (frac - 2.0) / 6.0,
        (frac + 1.0) * (frac - 1.0) * (frac - 2.0) / 2.0,
        -(frac + 1.0) * frac * (frac - 2.0) / 2.0,
        (frac + 1.0) * frac * (frac - 1.0) / 6.0,
    ]


def contribution(record, targets):
    steps_count = (record.shape[0] - 5) // 4
    values = record[: 4 * steps_count]
    places = record[4 * steps_count : 4 * steps_count + 3]
    delays = record[4 * steps_count + 3]
    weights = lagrange(record[4 * steps_count + 4])
    offset = jnp.arange(SAMPLES, dtype=jnp.float32)[None, :] - delays[:, None]
    banded = jnp.zeros((4, record.shape[1], SAMPLES), jnp.float32)
    for lag in range(steps_count + 3):
        summed = jnp.zeros((4, record.shape[1]), jnp.float32)
        for step in range(steps_count):
            tap = lag - step
            if 0 <= tap <= 3:
                summed = summed + values[4 * step : 4 * step + 4] * weights[tap][None]
        banded = banded + jnp.where((offset == lag)[None], summed[:, :, None], 0.0)
    apart = targets[:, :, None] - places[:, None, :]
    squared = apart[0] * apart[0] + apart[1] * apart[1] + apart[2] * apart[2] + 16.0
    radius = jnp.sqrt(squared)
    inverse = 4.0 / radius
    kernel = jnp.stack(
        [
            inverse,
            inverse * apart[0] / radius,
            inverse * apart[1] / radius,
            inverse * apart[2] / radius,
        ],
        axis=0,
    )
    return (kernel.astype(jnp.bfloat16), banded.astype(jnp.bfloat16))


def radiate(running, record, targets):
    kernel, banded = contribution(record, targets)
    return running + jnp.einsum("cop,cpt->ot", kernel, banded, preferred_element_type=jnp.float32)


def make_folder(targets, running, portion):
    row_count = portion.shape[1]
    blocks = portion.reshape(portion.shape[0], row_count // 512, 512).transpose(1, 0, 2)

    def add_block(acc, segment):
        return (radiate(acc, segment, targets), None)

    running, _ = lax.scan(add_block, running, blocks)
    return running


def per_device(flow_field, disk_mask, surf_cell, delay_bin, tap_phase, panel_counts, observer_pos):
    cfd_count = lax.axis_size("cfd")
    obs_count = lax.axis_size("obs")
    cfd_here = lax.axis_index("cfd")
    obs_here = lax.axis_index("obs")
    size_x, size_y, size_z = (flow_field.shape[1], flow_field.shape[2], flow_field.shape[3])
    mask_float = disk_mask.astype(jnp.float32)
    slots = surf_cell[0]
    slot_count = slots.shape[0]
    sampled = []
    state = flow_field
    for step in range(STEPS):
        padded = extended(state, (("cfd", 1), ("obs", 2)), 1)
        padded = jnp.pad(padded, ((0, 0), (0, 0), (0, 0), (1, 1)))
        state = advance(state, padded, mask_float)
        sampled.append(jnp.take(state.reshape(4, -1), slots, axis=1))
    glob_x = cfd_here * size_x + slots // (size_y * size_z)
    glob_y = obs_here * size_y + slots // size_z % size_y
    glob_z = slots % size_z
    extras = [
        glob_x.astype(jnp.float32)[None] + 0.5,
        glob_y.astype(jnp.float32)[None] + 0.5,
        glob_z.astype(jnp.float32)[None] + 0.5,
        delay_bin[0].astype(jnp.float32)[None],
        tap_phase[0].astype(jnp.float32)[None],
    ]
    record = jnp.concatenate(sampled + extras, axis=0)
    row_counts = lax.dynamic_index_in_dim(panel_counts, obs_here, 0, keepdims=False)
    owned = lax.dynamic_index_in_dim(row_counts, cfd_here, 0, keepdims=False)
    live = jnp.arange(slot_count) < owned
    record = jnp.where(live[None], record, 0.0)
    extents = jnp.array([size_x * cfd_count, size_y * obs_count, size_z], jnp.float32)
    targets = observer_pos * extents[:, None]
    initial = jnp.zeros((targets.shape[1], SAMPLES), jnp.float32)
    partial_signal = make_folder(
        targets, initial, lax.all_gather(record, "cfd", axis=1, tiled=True)
    )
    signal = lax.psum_scatter(partial_signal, "obs", scatter_dimension=0, tiled=True)
    return (state, signal)


def solution(mesh):
    return jax.shard_map(
        per_device,
        mesh=mesh,
        in_specs=(
            P(None, "cfd", "obs", None),
            P("cfd", "obs", None),
            P("obs", "cfd"),
            P("obs", "cfd"),
            P("obs", "cfd"),
            P(),
            P(None, "cfd"),
        ),
        out_specs=(P(None, "cfd", "obs", None), P(("cfd", "obs"), None)),
        check_vma=False,
    )
```

profile of v0, /device:TPU:1, one launch (start us, length us, event | category | flops | bytes accessed | tf_op | source)
XLA Modules:
  0.0 422.4 jit_solution(6125135691667169299)
XLA Ops:
  17.3 6.7 %collective-permute-start.2 = (f32[4,18,1,128]{3,2,1,0:T(1,128)S(1)}, f32[4,18,1,128]{3,2,1,0:T(1,128)S(1)}, u32[]{:S(2)}, u32[]{:S(2)}) collective-permute-start(f32[4,18,1,128]{3,2,1,0:T(1,128)S(1)} %get-tuple-element.113), channel_id=1, source_target_pairs={{1,0},{2,1},{3,2},{4,3},{5,4},{6,5},{7,6},{9,8},{10,9},{11,10},{12... | collective-permute-start | bytes 110600 | tf_op jit(solution)/shard_map/ppermute | solution.py:18
  59.2 8.5 %copy.46 = f32[4,32768]{0,1:T(8,128)} copy(f32[4,32768]{1,0:T(4,128)S(1)} %pad_maximum_fusion.44) | data formatting | bytes 1048576 | tf_op jit(solution)/shard_map/concatenate | solution.py:34
  67.7 6.4 %gather_fusion = f32[128,4]{1,0:T(8,128)S(1)} fusion(f32[4,32768]{0,1:T(8,128)} %copy.46, s32[1024]{0:T(1024)S(1)} %pad_clamp_fusion), kind=kCustom, calls=%fused_computation.clone | custom fusion | bytes 4608 | tf_op jit(solution)/shard_map/jit(_take)/gather | solution.py:109
  82.0 8.5 %copy.47 = f32[4,32768]{0,1:T(8,128)} copy(f32[4,32768]{1,0:T(4,128)S(1)} %pad_maximum_fusion.45) | data formatting | bytes 1048576 | tf_op jit(solution)/shard_map/concatenate | solution.py:34
  90.5 6.4 %gather_fusion.1 = f32[128,4]{1,0:T(8,128)S(1)} fusion(f32[4,32768]{0,1:T(8,128)} %copy.47, s32[1024]{0:T(1024)S(1)} %pad_clamp_fusion), kind=kCustom, calls=%fused_computation.1.clone | custom fusion | bytes 4608 | tf_op jit(solution)/shard_map/jit(_take)/gather | solution.py:109
  103.2 8.5 %copy.48 = f32[4,32768]{0,1:T(8,128)} copy(f32[4,32768]{1,0:T(4,128)S(1)} %pad_maximum_fusion.46) | data formatting | bytes 1048576 | tf_op jit(solution)/shard_map/concatenate | solution.py:34
  111.7 6.4 %gather_fusion.2 = f32[128,4]{1,0:T(8,128)S(1)} fusion(f32[4,32768]{0,1:T(8,128)} %copy.48, s32[1024]{0:T(1024)S(1)} %pad_clamp_fusion), kind=kCustom, calls=%fused_computation.2.clone | custom fusion | bytes 4608 | tf_op jit(solution)/shard_map/jit(_take)/gather | solution.py:109
  120.1 8.5 %copy.49 = f32[4,32768]{0,1:T(8,128)} copy(f32[4,32768]{1,0:T(4,128)S(1)} %pad_maximum_fusion.47) | data formatting | bytes 1048576 | tf_op jit(solution)/shard_map/concatenate | solution.py:34
  128.6 6.4 %gather_fusion.3 = f32[128,4]{1,0:T(8,128)S(1)} fusion(f32[4,32768]{0,1:T(8,128)} %copy.49, s32[1024]{0:T(1024)S(1)} %pad_clamp_fusion), kind=kCustom, calls=%fused_computation.3.clone | custom fusion | bytes 4608 | tf_op jit(solution)/shard_map/jit(_take)/gather | solution.py:109
  135.5 76.3 %all_gather.3 = f32[21,8192]{1,0:T(8,128)S(1)} all-gather(f32[21,128]{1,0:T(8,128)S(1)} %broadcast_select_fusion), channel_id=1, replica_groups=mesh['cfd'=64,'obs'=8] {'cfd'}, dimensions={1}, use_global_device_ids=true | all-gather | bytes 698880 | tf_op jit(solution)/shard_map/all_gather | solution.py:129
  212.8 155.6 %while.13 = (s32[]{:T(128)}, f32[128,512]{1,0:T(8,128)}, f32[3,128]{1,0:T(4,128)}, f32[16,21,512]{2,1,0:T(8,128)S(1)}, s32[]{:T(128)}, /*index=5*/s32[]{:T(128)}, s32[]{}, s32[]{}, s32[]{}, s32[]{}, /*index=10*/s32[]{}, s32[]{}) while((s32[]{:T(128)}, f32[128,512]{1,0:T(8,128)}, f32[3,128]{1,0:T(4,128)}, ...), condition=%wide.region_1.3_spmd.clone, body=%wide.region_0.2_spmd.clone.sunk | while | flops 287566848 | bytes 8322795 | solution.py:90
  226.5 5.6 %fusion.94 = f32[128,512]{1,0:T(8,128)} fusion(f32[4,512]{1,0:T(4,128)} %get-tuple-element.186, f32[4,512]{1,0:T(4,128)} %get-tuple-element.187, f32[4,512]{1,0:T(4,128)} %get-tuple-element.188, f32[4,512]{1,0:T(4,128)S(1)} %get-tuple-element.189, f32[4,512]{1,0:T(4,128)S(1)} %get-tuple-element.190, f32[4,512]{1,0:T(4,128)} %get-tuple-element.191, ...), kind=kOutput, calls=%fused_computation.14.clone.1 | convolution fusion | flops 284033024 | bytes 2940929 | tf_op jit(solution)/shard_map/while/body/eval_jaxpr/cop,cpt->ot/dot_general | solution.py:80
  245.9 5.6 %fusion.94 = f32[128,512]{1,0:T(8,128)} fusion(f32[4,512]{1,0:T(4,128)} %get-tuple-element.186, f32[4,512]{1,0:T(4,128)} %get-tuple-element.187, f32[4,512]{1,0:T(4,128)} %get-tuple-element.188, f32[4,512]{1,0:T(4,128)S(1)} %get-tuple-element.189, f32[4,512]{1,0:T(4,128)S(1)} %get-tuple-element.190, f32[4,512]{1,0:T(4,128)} %get-tuple-element.191, ...), kind=kOutput, calls=%fused_computation.14.clone.1 | convolution fusion | flops 284033024 | bytes 2940929 | tf_op jit(solution)/shard_map/while/body/eval_jaxpr/cop,cpt->ot/dot_general | solution.py:80
  255.7 5.6 %fusion.94 = f32[128,512]{1,0:T(8,128)} fusion(f32[4,512]{1,0:T(4,128)} %get-tuple-element.186, f32[4,512]{1,0:T(4,128)} %get-tuple-element.187, f32[4,512]{1,0:T(4,128)} %get-tuple-element.188, f32[4,512]{1,0:T(4,128)S(1)} %get-tuple-element.189, f32[4,512]{1,0:T(4,128)S(1)} %get-tuple-element.190, f32[4,512]{1,0:T(4,128)} %get-tuple-element.191, ...), kind=kOutput, calls=%fused_computation.14.clone.1 | convolution fusion | flops 284033024 | bytes 2940929 | tf_op jit(solution)/shard_map/while/body/eval_jaxpr/cop,cpt->ot/dot_general | solution.py:80
  265.4 5.6 %fusion.94 = f32[128,512]{1,0:T(8,128)} fusion(f32[4,512]{1,0:T(4,128)} %get-tuple-element.186, f32[4,512]{1,0:T(4,128)} %get-tuple-element.187, f32[4,512]{1,0:T(4,128)} %get-tuple-element.188, f32[4,512]{1,0:T(4,128)S(1)} %get-tuple-element.189, f32[4,512]{1,0:T(4,128)S(1)} %get-tuple-element.190, f32[4,512]{1,0:T(4,128)} %get-tuple-element.191, ...), kind=kOutput, calls=%fused_computation.14.clone.1 | convolution fusion | flops 284033024 | bytes 2940929 | tf_op jit(solution)/shard_map/while/body/eval_jaxpr/cop,cpt->ot/dot_general | solution.py:80
  275.2 5.6 %fusion.94 = f32[128,512]{1,0:T(8,128)} fusion(f32[4,512]{1,0:T(4,128)} %get-tuple-element.186, f32[4,512]{1,0:T(4,128)} %get-tuple-element.187, f32[4,512]{1,0:T(4,128)} %get-tuple-element.188, f32[4,512]{1,0:T(4,128)S(1)} %get-tuple-element.189, f32[4,512]{1,0:T(4,128)S(1)} %get-tuple-element.190, f32[4,512]{1,0:T(4,128)} %get-tuple-element.191, ...), kind=kOutput, calls=%fused_computation.14.clone.1 | convolution fusion | flops 284033024 | bytes 2940929 | tf_op jit(solution)/shard_map/while/body/eval_jaxpr/cop,cpt->ot/dot_general | solution.py:80
  284.9 5.6 %fusion.94 = f32[128,512]{1,0:T(8,128)} fusion(f32[4,512]{1,0:T(4,128)} %get-tuple-element.186, f32[4,512]{1,0:T(4,128)} %get-tuple-element.187, f32[4,512]{1,0:T(4,128)} %get-tuple-element.188, f32[4,512]{1,0:T(4,128)S(1)} %get-tuple-element.189, f32[4,512]{1,0:T(4,128)S(1)} %get-tuple-element.190, f32[4,512]{1,0:T(4,128)} %get-tuple-element.191, ...), kind=kOutput, calls=%fused_computation.14.clone.1 | convolution fusion | flops 284033024 | bytes 2940929 | tf_op jit(solution)/shard_map/while/body/eval_jaxpr/cop,cpt->ot/dot_general | solution.py:80
  304.4 5.6 %fusion.94 = f32[128,512]{1,0:T(8,128)} fusion(f32[4,512]{1,0:T(4,128)} %get-tuple-element.186, f32[4,512]{1,0:T(4,128)} %get-tuple-element.187, f32[4,512]{1,0:T(4,128)} %get-tuple-element.188, f32[4,512]{1,0:T(4,128)S(1)} %get-tuple-element.189, f32[4,512]{1,0:T(4,128)S(1)} %get-tuple-element.190, f32[4,512]{1,0:T(4,128)} %get-tuple-element.191, ...), kind=kOutput, calls=%fused_computation.14.clone.1 | convolution fusion | flops 284033024 | bytes 2940929 | tf_op jit(solution)/shard_map/while/body/eval_jaxpr/cop,cpt->ot/dot_general | solution.py:80
  314.1 5.6 %fusion.94 = f32[128,512]{1,0:T(8,128)} fusion(f32[4,512]{1,0:T(4,128)} %get-tuple-element.186, f32[4,512]{1,0:T(4,128)} %get-tuple-element.187, f32[4,512]{1,0:T(4,128)} %get-tuple-element.188, f32[4,512]{1,0:T(4,128)S(1)} %get-tuple-element.189, f32[4,512]{1,0:T(4,128)S(1)} %get-tuple-element.190, f32[4,512]{1,0:T(4,128)} %get-tuple-element.191, ...), kind=kOutput, calls=%fused_computation.14.clone.1 | convolution fusion | flops 284033024 | bytes 2940929 | tf_op jit(solution)/shard_map/while/body/eval_jaxpr/cop,cpt->ot/dot_general | solution.py:80
  333.6 5.6 %fusion.94 = f32[128,512]{1,0:T(8,128)} fusion(f32[4,512]{1,0:T(4,128)} %get-tuple-element.186, f32[4,512]{1,0:T(4,128)} %get-tuple-element.187, f32[4,512]{1,0:T(4,128)} %get-tuple-element.188, f32[4,512]{1,0:T(4,128)S(1)} %get-tuple-element.189, f32[4,512]{1,0:T(4,128)S(1)} %get-tuple-element.190, f32[4,512]{1,0:T(4,128)} %get-tuple-element.191, ...), kind=kOutput, calls=%fused_computation.14.clone.1 | convolution fusion | flops 284033024 | bytes 2940929 | tf_op jit(solution)/shard_map/while/body/eval_jaxpr/cop,cpt->ot/dot_general | solution.py:80
  343.3 5.6 %fusion.94 = f32[128,512]{1,0:T(8,128)} fusion(f32[4,512]{1,0:T(4,128)} %get-tuple-element.186, f32[4,512]{1,0:T(4,128)} %get-tuple-element.187, f32[4,512]{1,0:T(4,128)} %get-tuple-element.188, f32[4,512]{1,0:T(4,128)S(1)} %get-tuple-element.189, f32[4,512]{1,0:T(4,128)S(1)} %get-tuple-element.190, f32[4,512]{1,0:T(4,128)} %get-tuple-element.191, ...), kind=kOutput, calls=%fused_computation.14.clone.1 | convolution fusion | flops 284033024 | bytes 2940929 | tf_op jit(solution)/shard_map/while/body/eval_jaxpr/cop,cpt->ot/dot_general | solution.py:80
  353.1 5.6 %fusion.94 = f32[128,512]{1,0:T(8,128)} fusion(f32[4,512]{1,0:T(4,128)} %get-tuple-element.186, f32[4,512]{1,0:T(4,128)} %get-tuple-element.187, f32[4,512]{1,0:T(4,128)} %get-tuple-element.188, f32[4,512]{1,0:T(4,128)S(1)} %get-tuple-element.189, f32[4,512]{1,0:T(4,128)S(1)} %get-tuple-element.190, f32[4,512]{1,0:T(4,128)} %get-tuple-element.191, ...), kind=kOutput, calls=%fused_computation.14.clone.1 | convolution fusion | flops 284033024 | bytes 2940929 | tf_op jit(solution)/shard_map/while/body/eval_jaxpr/cop,cpt->ot/dot_general | solution.py:80
  362.8 5.6 %fusion.94 = f32[128,512]{1,0:T(8,128)} fusion(f32[4,512]{1,0:T(4,128)} %get-tuple-element.186, f32[4,512]{1,0:T(4,128)} %get-tuple-element.187, f32[4,512]{1,0:T(4,128)} %get-tuple-element.188, f32[4,512]{1,0:T(4,128)S(1)} %get-tuple-element.189, f32[4,512]{1,0:T(4,128)S(1)} %get-tuple-element.190, f32[4,512]{1,0:T(4,128)} %get-tuple-element.191, ...), kind=kOutput, calls=%fused_computation.14.clone.1 | convolution fusion | flops 284033024 | bytes 2940929 | tf_op jit(solution)/shard_map/while/body/eval_jaxpr/cop,cpt->ot/dot_general | solution.py:80
  370.2 45.3 %reduce-scatter.2.cloned.1.call-done = f32[16,512]{1,0:T(8,128)} async-done(((f32[128,512]{1,0:T(8,128)}), f32[16,512]{1,0:T(8,128)}) %reduce-scatter.2.cloned.1.call-update) | async-done | bytes 32784 | tf_op jit(solution)/shard_map/reduce_scatter | solution.py:131
  (233 shorter events, 151.9 us)
Async XLA Ops:
  7.2 408.4 %reduce-scatter.2.cloned.1.call-start = ((), (), s32[]{:S(2)}) async-start(), calls=%async_computation.1 | async-start | bytes 294912 | tf_op jit(solution)/shard_map/reduce_scatter | solution.py:131
  8.0 7.7 %collective-permute-start.1 = (f32[4,1,16,128]{3,2,1,0:T(8,128)S(1)}, f32[4,1,16,128]{3,2,1,0:T(8,128)S(1)}, u32[]{:S(2)}, u32[]{:S(2)}) collective-permute-start(f32[4,1,16,128]{3,2,1,0:T(8,128)S(1)} %get-tuple-element.121), channel_id=1, source_target_pairs={{0,8},{8,16},{16,24},{24,32},{32,40},{40,48},{48,56},{56,64},{64,7... | collective-permute-start | bytes 98312 | tf_op jit(solution)/shard_map/ppermute | solution.py:17
  12.4 4.8 %collective-permute-start = (f32[4,1,16,128]{3,2,1,0:T(8,128)S(1)}, f32[4,1,16,128]{3,2,1,0:T(8,128)S(1)}, u32[]{:S(2)}, u32[]{:S(2)}) collective-permute-start(f32[4,1,16,128]{3,2,1,0:T(8,128)S(1)} %get-tuple-element.120), channel_id=1, source_target_pairs={{8,0},{16,8},{24,16},{32,24},{40,32},{48,40},{56,48},{64,56},{72,6... | collective-permute-start | bytes 98312 | tf_op jit(solution)/shard_map/ppermute | solution.py:18
  15.7 12.2 %copy-start = (f32[4,16,16,128]{3,2,1,0:T(8,128)S(1)}, f32[4,16,16,128]{3,2,1,0:T(8,128)}, u32[]{:S(2)}) copy-start(f32[4,16,16,128]{3,2,1,0:T(8,128)} %param.12) | copy-start | bytes 1572868
  17.3 9.3 %collective-permute-start.2 = (f32[4,18,1,128]{3,2,1,0:T(1,128)S(1)}, f32[4,18,1,128]{3,2,1,0:T(1,128)S(1)}, u32[]{:S(2)}, u32[]{:S(2)}) collective-permute-start(f32[4,18,1,128]{3,2,1,0:T(1,128)S(1)} %get-tuple-element.113), channel_id=1, source_target_pairs={{1,0},{2,1},{3,2},{4,3},{5,4},{6,5},{7,6},{9,8},{10,9},{11,10},{12... | collective-permute-start | bytes 110600 | tf_op jit(solution)/shard_map/ppermute | solution.py:18
  23.9 3.1 collective-permute-start.3
  27.9 0.9 copy-start.1
  28.8 5.4 %copy-start.3 = (s32[1,128]{1,0:T(1,128)S(1)}, s32[1,128]{1,0:T(1,128)}, u32[]{:S(2)}) copy-start(s32[1,128]{1,0:T(1,128)} %param.14) | copy-start | bytes 1540
  28.9 5.3 %collective-permute-start.4 = (f32[4,1,16,128]{3,2,1,0:T(8,128)S(1)}, f32[4,1,16,128]{3,2,1,0:T(8,128)S(1)}, u32[]{:S(2)}, u32[]{:S(2)}) collective-permute-start(f32[4,1,16,128]{3,2,1,0:T(8,128)S(1)} %get-tuple-element.119), channel_id=1, source_target_pairs={{8,0},{16,8},{24,16},{32,24},{40,32},{48,40},{56,48},{64,56},{72,6... | collective-permute-start | bytes 98312 | tf_op jit(solution)/shard_map/ppermute | solution.py:18
  30.2 5.0 %collective-permute-start.5 = (f32[4,1,16,128]{3,2,1,0:T(8,128)S(1)}, f32[4,1,16,128]{3,2,1,0:T(8,128)S(1)}, u32[]{:S(2)}, u32[]{:S(2)}) collective-permute-start(f32[4,1,16,128]{3,2,1,0:T(8,128)S(1)} %get-tuple-element.118), channel_id=1, source_target_pairs={{0,8},{8,16},{16,24},{24,32},{32,40},{40,48},{48,56},{56,64},{64,7... | collective-permute-start | bytes 98312 | tf_op jit(solution)/shard_map/ppermute | solution.py:17
  35.3 8.5 %collective-permute-start.6 = (f32[4,18,1,128]{3,2,1,0:T(1,128)S(1)}, f32[4,18,1,128]{3,2,1,0:T(1,128)S(1)}, u32[]{:S(2)}, u32[]{:S(2)}) collective-permute-start(f32[4,18,1,128]{3,2,1,0:T(1,128)S(1)} %get-tuple-element.111), channel_id=1, source_target_pairs={{1,0},{2,1},{3,2},{4,3},{5,4},{6,5},{7,6},{9,8},{10,9},{11,10},{12... | collective-permute-start | bytes 110600 | tf_op jit(solution)/shard_map/ppermute | solution.py:18
  38.5 5.3 %collective-permute-start.7 = (f32[4,18,1,128]{3,2,1,0:T(1,128)S(1)}, f32[4,18,1,128]{3,2,1,0:T(1,128)S(1)}, u32[]{:S(2)}, u32[]{:S(2)}) collective-permute-start(f32[4,18,1,128]{3,2,1,0:T(1,128)S(1)} %get-tuple-element.110), channel_id=1, source_target_pairs={{0,1},{1,2},{2,3},{3,4},{4,5},{5,6},{6,7},{8,9},{9,10},{10,11},{11... | collective-permute-start | bytes 110600 | tf_op jit(solution)/shard_map/ppermute | solution.py:17
  45.1 6.7 %copy-start.4 = (s32[1,128]{1,0:T(1,128)S(1)}, s32[1,128]{1,0:T(1,128)}, u32[]{:S(2)}) copy-start(s32[1,128]{1,0:T(1,128)} %param.15) | copy-start | bytes 1540
  45.1 6.7 %copy-start.5 = (s32[1,128]{1,0:T(1,128)S(1)}, s32[1,128]{1,0:T(1,128)}, u32[]{:S(2)}) copy-start(s32[1,128]{1,0:T(1,128)} %param.16) | copy-start | bytes 1540
  45.2 6.9 %collective-permute-start.8 = (f32[4,1,16,128]{3,2,1,0:T(8,128)S(1)}, f32[4,1,16,128]{3,2,1,0:T(8,128)S(1)}, u32[]{:S(2)}, u32[]{:S(2)}) collective-permute-start(f32[4,1,16,128]{3,2,1,0:T(8,128)S(1)} %get-tuple-element.117), channel_id=1, source_target_pairs={{8,0},{16,8},{24,16},{32,24},{40,32},{48,40},{56,48},{64,56},{72,6... | collective-permute-start | bytes 98312 | tf_op jit(solution)/shard_map/ppermute | solution.py:18
  46.5 5.6 %collective-permute-start.9 = (f32[4,1,16,128]{3,2,1,0:T(8,128)S(1)}, f32[4,1,16,128]{3,2,1,0:T(8,128)S(1)}, u32[]{:S(2)}, u32[]{:S(2)}) collective-permute-start(f32[4,1,16,128]{3,2,1,0:T(8,128)S(1)} %get-tuple-element.116), channel_id=1, source_target_pairs={{0,8},{8,16},{16,24},{24,32},{32,40},{40,48},{48,56},{56,64},{64,7... | collective-permute-start | bytes 98312 | tf_op jit(solution)/shard_map/ppermute | solution.py:17
  52.2 22.2 %collective-permute-start.10 = (f32[4,18,1,128]{3,2,1,0:T(1,128)S(1)}, f32[4,18,1,128]{3,2,1,0:T(1,128)S(1)}, u32[]{:S(2)}, u32[]{:S(2)}) collective-permute-start(f32[4,18,1,128]{3,2,1,0:T(1,128)S(1)} %get-tuple-element.109), channel_id=1, source_target_pairs={{1,0},{2,1},{3,2},{4,3},{5,4},{6,5},{7,6},{9,8},{10,9},{11,10},{12... | collective-permute-start | bytes 110600 | tf_op jit(solution)/shard_map/ppermute | solution.py:18
  54.1 20.3 %collective-permute-start.11 = (f32[4,18,1,128]{3,2,1,0:T(1,128)S(1)}, f32[4,18,1,128]{3,2,1,0:T(1,128)S(1)}, u32[]{:S(2)}, u32[]{:S(2)}) collective-permute-start(f32[4,18,1,128]{3,2,1,0:T(1,128)S(1)} %get-tuple-element.108), channel_id=1, source_target_pairs={{0,1},{1,2},{2,3},{3,4},{4,5},{5,6},{6,7},{8,9},{9,10},{10,11},{11... | collective-permute-start | bytes 110600 | tf_op jit(solution)/shard_map/ppermute | solution.py:17
  75.8 21.3 %collective-permute-start.12 = (f32[4,1,16,128]{3,2,1,0:T(8,128)S(1)}, f32[4,1,16,128]{3,2,1,0:T(8,128)S(1)}, u32[]{:S(2)}, u32[]{:S(2)}) collective-permute-start(f32[4,1,16,128]{3,2,1,0:T(8,128)S(1)} %get-tuple-element.115), channel_id=1, source_target_pairs={{8,0},{16,8},{24,16},{32,24},{40,32},{48,40},{56,48},{64,56},{72,6... | collective-permute-start | bytes 98312 | tf_op jit(solution)/shard_map/ppermute | solution.py:18
  77.1 20.0 %collective-permute-start.13 = (f32[4,1,16,128]{3,2,1,0:T(8,128)S(1)}, f32[4,1,16,128]{3,2,1,0:T(8,128)S(1)}, u32[]{:S(2)}, u32[]{:S(2)}) collective-permute-start(f32[4,1,16,128]{3,2,1,0:T(8,128)S(1)} %get-tuple-element.114), channel_id=1, source_target_pairs={{0,8},{8,16},{16,24},{24,32},{32,40},{40,48},{48,56},{56,64},{64,7... | collective-permute-start | bytes 98312 | tf_op jit(solution)/shard_map/ppermute | solution.py:17
  97.2 20.9 %collective-permute-start.14 = (f32[4,18,1,128]{3,2,1,0:T(1,128)S(1)}, f32[4,18,1,128]{3,2,1,0:T(1,128)S(1)}, u32[]{:S(2)}, u32[]{:S(2)}) collective-permute-start(f32[4,18,1,128]{3,2,1,0:T(1,128)S(1)} %get-tuple-element.107), channel_id=1, source_target_pairs={{1,0},{2,1},{3,2},{4,3},{5,4},{6,5},{7,6},{9,8},{10,9},{11,10},{12... | collective-permute-start | bytes 110600 | tf_op jit(solution)/shard_map/ppermute | solution.py:18
  99.2 19.0 %collective-permute-start.15 = (f32[4,18,1,128]{3,2,1,0:T(1,128)S(1)}, f32[4,18,1,128]{3,2,1,0:T(1,128)S(1)}, u32[]{:S(2)}, u32[]{:S(2)}) collective-permute-start(f32[4,18,1,128]{3,2,1,0:T(1,128)S(1)} %get-tuple-element.106), channel_id=1, source_target_pairs={{0,1},{1,2},{2,3},{3,4},{4,5},{5,6},{6,7},{8,9},{9,10},{10,11},{11... | collective-permute-start | bytes 110600 | tf_op jit(solution)/shard_map/ppermute | solution.py:17
  119.6 9.0 %copy-start.2 = (f32[16,16,128]{2,1,0:T(8,128)}, f32[16,16,128]{2,1,0:T(8,128)S(1)}, u32[]{:S(2)}) copy-start(f32[16,16,128]{2,1,0:T(8,128)S(1)} %fusion.69) | copy-start | bytes 393220
Sparse Core Ops, SparseCore 0:
  368.6 46.9 reduce-scatter.1
where the time goes:
time: 425 us; the launch traced here: 422 us
  matrix products  89.5 us (21%)
  other arithmetic  77.5 us (18%)
  blocking collectives  76.3 us (18%)
  local copies, waits for them, and re-layouts  65.8 us (15%)
  starting transfers between devices  50.9 us (12%)
  waiting for transfers between devices  47.2 us (11%)
  between operations  14.6 us (3%)
    dot_general x16, matrix products, radiate(): jnp.einsum('cop,cpt->ot', kernel, banded, preferred_element_type=jnp.floa...  89.5 us
    all_gather x1, blocking collectives, per_device(): lax.all_gather(record, 'cfd', axis=1, tiled=True)  76.3 us
    reduce_scatter x1, waiting for transfers between devices, per_device(): lax.psum_scatter(partial_signal, 'obs', scatter_dimension=0, tiled=True)  45.3 us
    concatenate x4, local copies, waits for them, and re-layouts, advance(): return jnp.concatenate([pressure[None], velocity], axis=0)  34 us
    ppermute x8, starting transfers between devices, extended(): before = lax.ppermute(last, axis, up)  32 us
    eq x16, other arithmetic, contribution(): banded = banded + jnp.where((offset == lag)[None], summed[:, :, None], 0.0)  29.4 us
    gather x4, local copies, waits for them, and re-layouts, per_device(): sampled.append(jnp.take(state.reshape(4, -1), slots, axis=1))  25.7 us
    ppermute x8, starting transfers between devices, extended(): after = lax.ppermute(first, axis, down)  18.9 us
  transfers between devices with their start and end apart: 17, of which 4 were waited for; matrix products, arithmetic and copies ran while one was open for 13% of the time, Pallas kernels for 0%

commit v1 on v0

v1 whole, which is shorter than its diff:
```python
import functools

import jax
import jax.numpy as jnp
from jax import lax
from jax.experimental import pallas as pl
from jax.experimental.pallas import tpu as pltpu
from jax.sharding import PartitionSpec as P

STEPS = 4
SAMPLES = 512
SLOTS = 128
TARGETS = 128
CHUNK = 4
MESH = pl.DeviceIdType.MESH
F32 = jnp.float32
BF16 = jnp.bfloat16


def kernel(
    rings,
    flow,
    disk,
    cells,
    delays,
    phases,
    counts,
    spots,
    flow_out,
    signal,
    state,
    x_halo,
    y_halo,
    y_face,
    meta,
    values,
    onehot,
    towards,
    greens,
    bands,
    sums,
    whole,
    parts,
    x_send,
    x_recv,
    y_send,
    y_recv,
    meta_z_send,
    meta_z_recv,
    meta_y_send,
    meta_y_recv,
    val_z_send,
    val_z_recv,
    val_y_send,
    val_y_recv,
    part_send,
    part_recv,
):
    n_y, n_z, n_obs = rings
    n_cfd = n_y * n_z
    cfd = lax.axis_index("cfd")
    obs = lax.axis_index("obs")
    here_y = cfd // n_z
    here_z = cfd % n_z
    size_x, size_y, size_z = flow.shape[1:]
    owned = TARGETS // n_obs

    def along_z(far):
        return here_y * n_z + lax.rem(here_z + far, n_z)

    def along_y(far):
        return lax.rem(here_y + far, n_y) * n_z + here_z

    def along_obs(far):
        return lax.rem(obs + far, n_obs)

    cfd_next, cfd_prev = lax.rem(cfd + 1, n_cfd), lax.rem(cfd + n_cfd - 1, n_cfd)
    obs_next, obs_prev = along_obs(1), along_obs(n_obs - 1)

    barrier = pltpu.get_barrier_semaphore()

    def greet(to_cfd, to_obs):
        pl.semaphore_signal(barrier, inc=1, device_id=(to_cfd, to_obs), device_id_type=MESH)

    for far in range(1, n_z):
        greet(along_z(far), obs)
    for far in range(1, n_y):
        greet(along_y(far), obs)
    for far in range(1, n_obs):
        greet(cfd, along_obs(far))
    greet(cfd_next, obs)
    greet(cfd_prev, obs)

    cell = cells[...]
    row_of = cell >> 7
    z_of = cell & 127
    phase = phases[...].astype(F32) * 0.25
    live_at = (lax.broadcasted_iota(jnp.int32, counts.shape, 0) == obs) & (
        lax.broadcasted_iota(jnp.int32, counts.shape, 1) == cfd
    )
    own = jnp.sum(jnp.where(live_at, counts[...], 0).astype(F32), axis=(0, 1), keepdims=True)
    live = lax.broadcasted_iota(jnp.int32, (1, SLOTS), 1).astype(F32) < own
    meta[cfd] = jnp.concatenate(
        [
            (cfd * size_x + (cell >> 11)).astype(F32) + 0.5,
            (obs * size_y + (row_of & 15)).astype(F32) + 0.5,
            z_of.astype(F32) + 0.5,
            delays[...].astype(F32),
            -phase * (phase - 1.0) * (phase - 2.0) / 6.0,
            (phase + 1.0) * (phase - 1.0) * (phase - 2.0) / 2.0,
            -(phase + 1.0) * phase * (phase - 2.0) / 2.0,
            (phase + 1.0) * phase * (phase - 1.0) / 6.0,
        ],
        axis=0,
    )
    onehot[...] = jnp.where(
        lax.broadcasted_iota(jnp.int32, (size_x * size_y, SLOTS), 0) == row_of, 1.0, 0.0
    ).astype(BF16)
    z_at = lax.broadcasted_iota(jnp.int32, (size_z, SLOTS), 0) == z_of

    row = lax.broadcasted_iota(jnp.int32, (size_y, size_z), 0)
    lane = lax.broadcasted_iota(jnp.int32, (size_y, size_z), 1)

    def fields(step):
        if step == 0:
            return flow
        return flow_out if step == STEPS else state.at[step - 1]

    def x_copy(step, side):
        edge = size_x - 1 if side == 0 else 0
        return pltpu.make_async_remote_copy(
            src_ref=fields(step).at[:, edge],
            dst_ref=x_halo.at[step, side],
            send_sem=x_send.at[step, side],
            recv_sem=x_recv.at[step, side],
            device_id=(cfd_next if side == 0 else cfd_prev, obs),
            device_id_type=MESH,
        )

    def y_copy(step, side):
        return pltpu.make_async_remote_copy(
            src_ref=y_face.at[step, side],
            dst_ref=y_halo.at[step, side],
            send_sem=y_send.at[step, side],
            recv_sem=y_recv.at[step, side],
            device_id=(cfd, obs_next if side == 0 else obs_prev),
            device_id_type=MESH,
        )

    def halo_start(step):
        for side in range(2):
            y_copy(step, side).start()
            x_copy(step, side).start()

    def halo_wait(step):
        for side in range(2):
            y_copy(step, side).wait()
            x_copy(step, side).wait()

    def faces(step):
        ref = fields(step)

        @pl.loop(0, size_x)
        def _(i):
            for c in range(4):
                y_face[step, 0, c, pl.ds(i, 1), :] = ref[c, i, size_y - 1 : size_y, :]
                y_face[step, 1, c, pl.ds(i, 1), :] = ref[c, i, 0:1, :]

    def main(step):
        ref, new = fields(step), fields(step + 1)

        @pl.loop(0, size_x)
        def _(i):
            disk_here = disk[i].astype(F32)
            below = jnp.where(i > 0, 0.4, 0.0)
            above = jnp.where(i < size_x - 1, 0.1, 0.0)
            before = jnp.maximum(i - 1, 0)
            after = jnp.minimum(i + 1, size_x - 1)
            slabs = [ref[c, i] for c in range(4)]
            for c in range(4):
                q = slabs[c]
                near = (
                    q
                    + jnp.where(row == 0, 0.0, pltpu.roll(q, 1, 0))
                    + jnp.where(row == size_y - 1, 0.0, pltpu.roll(q, size_y - 1, 0))
                    + jnp.where(lane == 0, 0.0, pltpu.roll(q, 1, 1))
                    + jnp.where(lane == size_z - 1, 0.0, pltpu.roll(q, size_z - 1, 1))
                )
                moved = 0.1 * near + below * ref[c, before] + above * ref[c, after]
                pull = 0.5 * slabs[1] if c == 0 else -0.4 * q
                new[c, i] = moved + disk_here * pull

    def fix(step):
        new = fields(step + 1)
        x_low = jnp.where(cfd > 0, 0.4, 0.0)
        x_high = jnp.where(cfd < n_cfd - 1, 0.1, 0.0)
        y_low = jnp.where(obs > 0, 0.1, 0.0)
        y_high = jnp.where(obs < n_obs - 1, 0.1, 0.0)
        for c in range(4):
            new[c, 0] = new[c, 0] + x_low * x_halo[step, 0, c]
            new[c, size_x - 1] = new[c, size_x - 1] + x_high * x_halo[step, 1, c]

        @pl.loop(0, size_x)
        def _(i):
            for c in range(4):
                low = y_low * y_halo[step, 0, c, pl.ds(i, 1), :]
                high = y_high * y_halo[step, 1, c, pl.ds(i, 1), :]
                slab = new[c, i] + jnp.where(
                    row == 0, low, jnp.where(row == size_y - 1, high, 0.0)
                )
                new[c, i] = slab
                if step + 1 < STEPS:
                    y_face[step + 1, 0, c, pl.ds(i, 1), :] = slab[size_y - 1 : size_y]
                    y_face[step + 1, 1, c, pl.ds(i, 1), :] = slab[0:1]

    def sample(step):
        new = fields(step + 1)
        for c in range(4):
            q = new[c].reshape(size_x * size_y, size_z)
            high = q.astype(BF16)
            low = (q - high.astype(F32)).astype(BF16)
            dims = (((0,), (0,)), ((), ()))
            lines = lax.dot_general(high, onehot[...], dims, preferred_element_type=F32)
            lines = lines + lax.dot_general(low, onehot[...], dims, preferred_element_type=F32)
            v = jnp.sum(jnp.where(z_at, lines, 0.0), axis=0, keepdims=True)
            values[step, cfd, c : c + 1, :] = jnp.where(live, v, 0.0)

    def z_copy(buf, block, send, recv, far, source):
        return pltpu.make_async_remote_copy(
            src_ref=buf.at[block],
            dst_ref=buf.at[block],
            send_sem=send.at[far],
            recv_sem=recv.at[source],
            device_id=(along_z(far), obs),
            device_id_type=MESH,
        )

    def z_start(buf, send, recv):
        @pl.loop(1, n_z)
        def _(far):
            z_copy(buf, cfd, send, recv, far, far).start()

    def z_wait(buf, send, recv):
        @pl.loop(1, n_z)
        def _(far):
            z_copy(buf, cfd, send, recv, far, far).wait_send()
            source = here_y * n_z + lax.rem(here_z + n_z - far, n_z)
            z_copy(buf, source, send, recv, far, far).wait_recv()

    def y_group(buf, group, send, recv, far):
        block = pl.ds(pl.multiple_of(group * n_z, n_z), n_z)
        return pltpu.make_async_remote_copy(
            src_ref=buf.at[block],
            dst_ref=buf.at[block],
            send_sem=send.at[far],
            recv_sem=recv.at[far],
            device_id=(along_y(far), obs),
            device_id_type=MESH,
        )

    def group_at(back):
        return lax.rem(here_y + n_y - back, n_y)

    def y_start(buf, send, recv):
        for far in range(1, n_y):
            y_group(buf, here_y, send, recv, far).start()

    def y_wait_recv(buf, send, recv, far):
        y_group(buf, group_at(far), send, recv, far).wait_recv()

    def y_wait_send(buf, send, recv):
        for far in range(1, n_y):
            y_group(buf, here_y, send, recv, far).wait_send()

    def prepare(group):
        @pl.loop(0, n_z)
        def _(k):
            block = group * n_z + k
            rows = meta[block]
            for first in range(0, TARGETS, 32):
                part = pl.ds(first, 32)
                d = [towards[a, part, :] - rows[a : a + 1] for a in range(3)]
                inv = lax.rsqrt(d[0] * d[0] + d[1] * d[1] + d[2] * d[2] + 16.0)
                four = 4.0 * inv
                square = four * inv
                greens[block, 0, part, :] = four
                for a in range(3):
                    greens[block, a + 1, part, :] = square * d[a]
            for first in range(0, SAMPLES, 64):
                at = (lax.broadcasted_iota(jnp.int32, (64, SLOTS), 0) + first).astype(F32)
                band = jnp.zeros((64, SLOTS), F32)
                for tap in range(4):
                    band = jnp.where(at == rows[3:4] + float(tap), rows[4 + tap : 5 + tap], band)
                bands[block, pl.ds(first, 64), :] = band.astype(BF16)

    def radiate(group, steps):
        many = min(CHUNK, n_z)

        @pl.loop(0, n_z // many)
        def _(k):
            start = group * n_z + k * many
            lhs = jnp.concatenate([bands[start + j] for j in range(many)], axis=1)
            columns = []
            for j in range(many):
                pieces = []
                for step in steps:
                    v = values[step, start + j]
                    for first in range(0, TARGETS, 32):
                        part = pl.ds(first, 32)
                        term = greens[start + j, 0, part, :] * v[0:1]
                        for c in range(1, 4):
                            term = term + greens[start + j, c, part, :] * v[c : c + 1]
                        pieces.append(term.astype(BF16))
                columns.append(jnp.concatenate(pieces, axis=0))
            rhs = jnp.concatenate(columns, axis=1)
            out = lax.dot_general(lhs, rhs, (((1,), (1,)), ((), ())), preferred_element_type=F32)
            for at, step in enumerate(steps):
                sums[step] += out[:, at * TARGETS : (at + 1) * TARGETS]

    def meta_refs():
        return (meta, meta_z_send, meta_z_recv)

    def meta_y_refs():
        return (meta, meta_y_send, meta_y_recv)

    def val_refs(step):
        return (values.at[step], val_z_send.at[step], val_z_recv.at[step])

    def val_y_refs(step):
        return (values.at[step], val_y_send.at[step], val_y_recv.at[step])

    faces(0)
    pl.semaphore_wait(barrier, n_z - 1 + n_y - 1 + n_obs - 1 + 2)

    halo_start(0)
    z_start(*meta_refs())
    extent = (size_x * n_cfd, size_y * n_obs, size_z)
    for a in range(3):
        line = spots[a : a + 1] * float(extent[a])
        towards[a] = jnp.transpose(jnp.broadcast_to(line, (SLOTS, TARGETS)))
    sums[...] = jnp.zeros_like(sums)
    main(0)
    halo_wait(0)
    fix(0)
    halo_start(1)
    sample(0)
    z_start(*val_refs(0))
    main(1)
    z_wait(*meta_refs())
    y_start(*meta_y_refs())
    prepare(here_y)
    halo_wait(1)
    fix(1)
    halo_start(2)
    sample(1)
    z_start(*val_refs(1))
    main(2)
    z_wait(*val_refs(0))
    y_start(*val_y_refs(0))
    if n_y > 1:
        y_wait_recv(*meta_y_refs(), 1)
        prepare(group_at(1))
    halo_wait(2)
    fix(2)
    halo_start(3)
    sample(2)
    z_start(*val_refs(2))
    main(3)
    z_wait(*val_refs(1))
    y_start(*val_y_refs(1))
    if n_y > 2:
        y_wait_recv(*meta_y_refs(), 2)
        prepare(group_at(2))
    halo_wait(3)
    fix(3)
    sample(3)
    z_start(*val_refs(3))
    z_wait(*val_refs(2))
    y_start(*val_y_refs(2))
    for far in range(3, n_y):
        y_wait_recv(*meta_y_refs(), far)
        prepare(group_at(far))
    z_wait(*val_refs(3))
    y_start(*val_y_refs(3))
    y_wait_send(*meta_y_refs())
    for far in range(n_y):
        if far > 0:
            y_wait_recv(*val_y_refs(0), far)
            y_wait_recv(*val_y_refs(1), far)
        radiate(group_at(far), (0, 1))
    for far in range(n_y):
        if far > 0:
            y_wait_recv(*val_y_refs(2), far)
            y_wait_recv(*val_y_refs(3), far)
        radiate(group_at(far), (2, 3))
    for step in range(STEPS):
        y_wait_send(*val_y_refs(step))

    total = sums[0]
    for step in range(1, STEPS):
        total = total + pltpu.roll(sums[step], step, 0)
    whole[...] = jnp.transpose(total)

    def part_copy(far):
        return pltpu.make_async_remote_copy(
            src_ref=whole.at[pl.ds(pl.multiple_of(along_obs(far) * owned, owned), owned)],
            dst_ref=parts.at[far - 1],
            send_sem=part_send.at[far - 1],
            recv_sem=part_recv.at[far - 1],
            device_id=(cfd, along_obs(far)),
            device_id_type=MESH,
        )

    for far in range(1, n_obs):
        part_copy(far).start()
    result = whole[pl.ds(pl.multiple_of(obs * owned, owned), owned), :]
    for far in range(1, n_obs):
        part_copy(far).wait()
        result = result + parts[far - 1]
    signal[...] = result


def per_device(rings, flow_field, disk_mask, surf_cell, delay_bin, tap_phase, panel_counts, observer_pos):
    n_y, n_z, n_obs = rings
    n_cfd = n_y * n_z
    _, size_x, size_y, size_z = flow_field.shape
    owned = TARGETS // n_obs
    dma = pltpu.SemaphoreType.DMA
    vmem = pl.BlockSpec(memory_space=pltpu.VMEM)
    return pl.pallas_call(
        functools.partial(kernel, rings),
        out_shape=(
            jax.ShapeDtypeStruct(flow_field.shape, F32),
            jax.ShapeDtypeStruct((owned, SAMPLES), F32),
        ),
        in_specs=[vmem] * 7,
        out_specs=(vmem, vmem),
        scratch_shapes=[
            pltpu.VMEM((STEPS - 1,) + flow_field.shape, F32),
            pltpu.VMEM((STEPS, 2, 4, size_y, size_z), F32),
            pltpu.VMEM((STEPS, 2, 4, size_x, size_z), F32),
            pltpu.VMEM((STEPS, 2, 4, size_x, size_z), F32),
            pltpu.VMEM((n_cfd, 8, SLOTS), F32),
            pltpu.VMEM((STEPS, n_cfd, 4, SLOTS), F32),
            pltpu.VMEM((size_x * size_y, SLOTS), BF16),
            pltpu.VMEM((3, TARGETS, SLOTS), F32),
            pltpu.VMEM((n_cfd, 4, TARGETS, SLOTS), F32),
            pltpu.VMEM((n_cfd, SAMPLES, SLOTS), BF16),
            pltpu.VMEM((STEPS, SAMPLES, TARGETS), F32),
            pltpu.VMEM((TARGETS, SAMPLES), F32),
            pltpu.VMEM((n_obs - 1, owned, SAMPLES), F32),
            dma((STEPS, 2)),
            dma((STEPS, 2)),
            dma((STEPS, 2)),
            dma((STEPS, 2)),
            dma((n_z,)),
            dma((n_z,)),
            dma((n_y,)),
            dma((n_y,)),
            dma((STEPS, n_z)),
            dma((STEPS, n_z)),
            dma((STEPS, n_y)),
            dma((STEPS, n_y)),
            dma((n_obs - 1,)),
            dma((n_obs - 1,)),
        ],
        compiler_params=pltpu.CompilerParams(
            collective_id=0, has_side_effects=True, vmem_limit_bytes=48 * 1024 * 1024
        ),
    )(flow_field, disk_mask, surf_cell, delay_bin, tap_phase, panel_counts, observer_pos)


def solution(mesh):
    n_cfd, n_obs = mesh.shape["cfd"], mesh.shape["obs"]
    n_y = 4 if n_cfd >= 16 else 2
    rings = (n_y, n_cfd // n_y, n_obs)
    return jax.shard_map(
        functools.partial(per_device, rings),
        mesh=mesh,
        in_specs=(
            P(None, "cfd", "obs", None),
            P("cfd", "obs", None),
            P("obs", "cfd"),
            P("obs", "cfd"),
            P("obs", "cfd"),
            P(),
            P(None, "cfd"),
        ),
        out_specs=(P(None, "cfd", "obs", None), P(("cfd", "obs"), None)),
        check_vma=False,
    )
```

time: 425 us -> 72.8 us (0.17)
  matrix products: 89.5 us -> 0 us
  other arithmetic: 77.5 us -> 0 us
  blocking collectives: 76.3 us -> 0 us
  Pallas kernels: 0 us -> 65.2 us
  local copies, waits for them, and re-layouts: 65.8 us -> 6.68 us
  starting transfers between devices: 50.9 us -> 0 us
  waiting for transfers between devices: 47.2 us -> 0 us
  between operations: 14.6 us -> 0.66 us
    dot_general x16 -> x0, matrix products: 89.5 us -> none  [radiate(): jnp.einsum('cop,cpt->ot', kernel, banded, preferred_element_type=jnp.floa...]
    all_gather x1 -> x0, blocking collectives: 76.3 us -> none  [per_device(): lax.all_gather(record, 'cfd', axis=1, tiled=True)]
    pallas_call x0 -> x1, Pallas kernels: none -> 65.2 us  [per_device(): pl.pallas_call(functools.partial(kernel, rings), out_shape=(jax.ShapeDtyp...]
    ppermute x16 -> x0, starting transfers between devices: 50.9 us -> none  [the longest x8 32 us: extended(): before = lax.ppermute(last, axis, up)]
    reduce_scatter x1 -> x0, waiting for transfers between devices: 45.3 us -> none  [per_device(): lax.psum_scatter(partial_signal, 'obs', scatter_dimension=0, tiled=True)]
    concatenate x6 -> x0, local copies, waits for them, and re-layouts: 34 us -> none  [the longest x4 34 us: advance(): return jnp.concatenate([pressure[None], velocity], axis=0)]
    eq x16 -> x0, other arithmetic: 29.4 us -> none  [contribution(): banded = banded + jnp.where((offset == lag)[None], summed[:, :, None], 0.0)]
    gather x4 -> x0, local copies, waits for them, and re-layouts: 25.7 us -> none  [per_device(): sampled.append(jnp.take(state.reshape(4, -1), slots, axis=1))]
  transfers between devices with their start and end apart: 17 -> 0, of which waited for: 4 -> 0; matrix products, arithmetic and copies ran while one was open for 13% -> 0% of each run, Pallas kernels for 0% -> 0%
where the time goes in v1:
time: 72.8 us; the launch traced here: 72.6 us
  Pallas kernels  65.2 us (90%)
  local copies, waits for them, and re-layouts  6.68 us (9%)
    pallas_call x1, Pallas kernels, per_device(): pl.pallas_call(functools.partial(kernel, rings), out_shape=(jax.ShapeDtyp...  65.2 us
    unnamed x16, local copies, waits for them, and re-layouts  6.68 us

profile of v1, /device:TPU:1, one launch (start us, length us, event | category | flops | bytes accessed | tf_op | source)
XLA Modules:
  0.0 72.6 jit_solution(12933723662824685804)
XLA Ops:
  0.6 0.0 copy-start
  0.6 1.0 %copy-done = f32[4,16,16,128]{3,2,1,0:T(8,128)S(1)} copy-done((f32[4,16,16,128]{3,2,1,0:T(8,128)S(1)}, f32[4,16,16,128]{3,2,1,0:T(8,128)}, u32[]{:S(2)}) %copy-start) | copy-done | bytes 524312
  1.7 0.0 copy-start.1
  1.7 0.9 %copy-done.1 = s32[16,16,128]{2,1,0:T(8,128)S(1)} copy-done((s32[16,16,128]{2,1,0:T(8,128)S(1)}, s32[16,16,128]{2,1,0:T(8,128)}, u32[]{:S(2)}) %copy-start.1) | copy-done | bytes 131096
  2.6 0.0 copy-start.2
  2.6 0.7 copy-done.2
  3.3 0.0 copy-start.3
  3.3 0.7 copy-done.3
  3.9 0.0 copy-start.4
  4.0 0.7 copy-done.4
  4.6 0.0 copy-start.5
  4.6 0.7 copy-done.5
  5.3 0.0 copy-start.6
  5.3 0.7 copy-done.6
  5.9 65.2 %shard_map.86 = (f32[4,16,16,128]{3,2,1,0:T(8,128)S(1)}, f32[16,512]{1,0:T(8,128)S(1)}) custom-call(f32[4,16,16,128]{3,2,1,0:T(8,128)S(1)} %copy-done, s32[16,16,128]{2,1,0:T(8,128)S(1)} %copy-done.1, s32[1,128]{1,0:T(1,128)S(1)} %copy-done.4, s32[1,128]{1,0:T(1,128)S(1)} %copy-done.5, s32[1,128]{1,0:T(1,128)S(1)} %copy-done.6, s32[8,64]{1,0:T(8,128)S(1)} %copy-done.2, ...), custom_call_target="tpu_custom_call" | custom-call | tf_op jit(solution)/shard_map/pallas_call | solution.py:430
  71.2 0.8 %copy.11 = f32[4,16,16,128]{3,2,1,0:T(8,128)} copy(f32[4,16,16,128]{3,2,1,0:T(8,128)S(1)} %get-tuple-element.4) | data formatting | bytes 1048576
  72.0 0.6 copy.12
Async XLA Ops:
  0.6 1.0 %copy-start = (f32[4,16,16,128]{3,2,1,0:T(8,128)S(1)}, f32[4,16,16,128]{3,2,1,0:T(8,128)}, u32[]{:S(2)}) copy-start(f32[4,16,16,128]{3,2,1,0:T(8,128)} %flow.1) | copy-start | bytes 1572868
  1.7 0.9 %copy-start.1 = (s32[16,16,128]{2,1,0:T(8,128)S(1)}, s32[16,16,128]{2,1,0:T(8,128)}, u32[]{:S(2)}) copy-start(s32[16,16,128]{2,1,0:T(8,128)} %disk.1) | copy-start | bytes 393220
  2.6 0.7 copy-start.2
  3.3 0.7 copy-start.3
  3.9 0.7 copy-start.4
  4.6 0.7 copy-start.5
  5.3 0.7 copy-start.6

commit v2 on v1

v2 whole, which is shorter than its diff:
```python
import functools

import jax
import jax.numpy as jnp
from jax import lax
from jax.experimental import pallas as pl
from jax.experimental.pallas import tpu as pltpu
from jax.sharding import PartitionSpec as P

STEPS = 4
SAMPLES = 512
SLOTS = 128
TARGETS = 128
WIDTH = 4
SIDE = 8
MESH = pl.DeviceIdType.MESH
F32 = jnp.float32
BF16 = jnp.bfloat16


def kernel(
    rings,
    flow_in,
    disk_in,
    cells_in,
    delays_in,
    phases_in,
    counts_in,
    spots_in,
    flow_out,
    signal,
    disk,
    cells,
    delays,
    phases,
    counts,
    spots,
    in_sem,
    wide,
    state,
    last,
    meta,
    values,
    onehot,
    towards,
    greens,
    bands,
    sums,
    whole,
    parts,
    halo_send,
    halo_recv,
    meta_z_send,
    meta_z_recv,
    meta_y_send,
    meta_y_recv,
    val_z_send,
    val_z_recv,
    val_y_send,
    val_y_recv,
    part_send,
    part_recv,
):
    n_y, n_z, n_obs = rings
    n_cfd = n_y * n_z
    cfd = lax.axis_index("cfd")
    obs = lax.axis_index("obs")
    here_y = cfd // n_z
    here_z = cfd % n_z
    size_x, size_y, size_z = flow_in.shape[1:]
    owned = TARGETS // n_obs
    own_x = slice(WIDTH, WIDTH + size_x)
    own_y = slice(SIDE, SIDE + size_y)
    tall = size_y + 2 * SIDE

    def along_z(far):
        return here_y * n_z + lax.rem(here_z + far, n_z)

    def along_y(far):
        return lax.rem(here_y + far, n_y) * n_z + here_z

    def along_obs(far):
        return lax.rem(obs + far, n_obs)

    cfd_next, cfd_prev = lax.rem(cfd + 1, n_cfd), lax.rem(cfd + n_cfd - 1, n_cfd)
    obs_next, obs_prev = along_obs(1), along_obs(n_obs - 1)

    inputs = [
        pltpu.make_async_copy(src, dst, in_sem.at[i])
        for i, (src, dst) in enumerate(
            [
                (disk_in, disk),
                (flow_in, wide.at[0:4, own_x, own_y]),
                (cells_in, cells),
                (delays_in, delays),
                (phases_in, phases),
                (counts_in, counts),
                (spots_in, spots),
            ]
        )
    ]
    for copy in inputs:
        copy.start()

    barrier = pltpu.get_barrier_semaphore()

    def greet(to_cfd, to_obs):
        pl.semaphore_signal(barrier, inc=1, device_id=(to_cfd, to_obs), device_id_type=MESH)

    for to_cfd in (cfd_next, cfd_prev):
        for to_obs in (obs_next, obs_prev, obs):
            greet(to_cfd, to_obs)
    for far in range(1, n_z):
        greet(along_z(far), obs)
    for far in range(1, n_y):
        greet(along_y(far), obs)
    for far in range(1, n_obs):
        greet(cfd, along_obs(far))

    inputs[0].wait()
    for i in range(size_x):
        wide[4, WIDTH + i, own_y] = disk[i].astype(F32)
    for copy in inputs[1:]:
        copy.wait()

    cell = cells[...]
    row_of = cell >> 7
    live_at = (lax.broadcasted_iota(jnp.int32, counts.shape, 0) == obs) & (
        lax.broadcasted_iota(jnp.int32, counts.shape, 1) == cfd
    )
    own = jnp.sum(jnp.where(live_at, counts[...], 0).astype(F32), axis=(0, 1), keepdims=True)
    live = lax.broadcasted_iota(jnp.int32, (1, SLOTS), 1).astype(F32) < own
    meta[cfd] = jnp.concatenate(
        [
            cell.astype(F32),
            delays[...].astype(F32),
            phases[...].astype(F32),
            jnp.zeros((1, SLOTS), F32),
        ],
        axis=0,
    )
    pl.semaphore_wait(barrier, 6 + n_z - 1 + n_y - 1 + n_obs - 1)

    def halo_copies():
        low_x, high_x = slice(0, WIDTH), slice(WIDTH + size_x, 2 * WIDTH + size_x)
        low_y, high_y = slice(0, SIDE), slice(SIDE + size_y, tall)
        first_x, last_x = slice(WIDTH, 2 * WIDTH), slice(size_x, size_x + WIDTH)
        first_y, last_y = slice(SIDE, 2 * SIDE), slice(size_y, size_y + SIDE)
        low_c, high_c = slice(1, WIDTH), slice(WIDTH + size_x, 2 * WIDTH + size_x - 1)
        first_c, last_c = slice(WIDTH, 2 * WIDTH - 1), slice(size_x + 1, size_x + WIDTH)
        moves = [
            (last_x, own_y, low_x, own_y, cfd_next, obs),
            (first_x, own_y, high_x, own_y, cfd_prev, obs),
            (last_c, last_y, low_c, low_y, cfd_next, obs_next),
            (last_c, first_y, low_c, high_y, cfd_next, obs_prev),
            (first_c, last_y, high_c, low_y, cfd_prev, obs_next),
            (first_c, first_y, high_c, high_y, cfd_prev, obs_prev),
            (own_x, last_y, own_x, low_y, cfd, obs_next),
            (own_x, first_y, own_x, high_y, cfd, obs_prev),
        ]
        return [
            pltpu.make_async_remote_copy(
                src_ref=wide.at[:, from_x, from_y],
                dst_ref=wide.at[:, to_x, to_y],
                send_sem=halo_send.at[i],
                recv_sem=halo_recv.at[i],
                device_id=(to_cfd, to_obs),
                device_id_type=MESH,
            )
            for i, (from_x, from_y, to_x, to_y, to_cfd, to_obs) in enumerate(moves)
        ]

    def fields(step):
        return wide if step == 0 else state.at[step - 1]

    def outside(step):
        ref = fields(step)

        @pl.when(cfd == 0)
        def _():
            ref[0:4, 0:WIDTH] = jnp.zeros((4, WIDTH, tall, size_z), F32)

        @pl.when(cfd == n_cfd - 1)
        def _():
            ref[0:4, WIDTH + size_x :] = jnp.zeros((4, WIDTH, tall, size_z), F32)

        @pl.when(obs == 0)
        def _():
            ref[0:4, :, 0:SIDE] = jnp.zeros((4, size_x + 2 * WIDTH, SIDE, size_z), F32)

        @pl.when(obs == n_obs - 1)
        def _():
            ref[0:4, :, SIDE + size_y :] = jnp.zeros((4, size_x + 2 * WIDTH, SIDE, size_z), F32)

    lane = lax.broadcasted_iota(jnp.int32, (tall, size_z), 1)

    def advance(step):
        ref = fields(step)
        final = step == STEPS - 1

        @pl.loop(1 + step, 2 * WIDTH + size_x - 1 - step, unroll=True)
        def _(i):
            slabs = [ref[c, i] for c in range(4)]
            there = wide[4, i]
            for c in range(4):
                q = slabs[c]
                near = (
                    q
                    + ref[c, i + 1]
                    + pltpu.roll(q, 1, 0)
                    + pltpu.roll(q, tall - 1, 0)
                    + jnp.where(lane == 0, 0.0, pltpu.roll(q, 1, 1))
                    + jnp.where(lane == size_z - 1, 0.0, pltpu.roll(q, size_z - 1, 1))
                )
                pull = 0.5 * slabs[1] if c == 0 else -0.4 * q
                moved = 0.1 * near + 0.4 * ref[c, i - 1] + there * pull
                if final:
                    last[c, i - WIDTH] = moved[own_y]
                else:
                    state[step, c, i] = moved

    def sample(step):
        for c in range(4):
            block = last[c] if step == STEPS - 1 else state[step, c, own_x, own_y]
            q = block.reshape(size_x * size_y, size_z)
            high = q.astype(BF16)
            low = (q - high.astype(F32)).astype(BF16)
            dims = (((0,), (0,)), ((), ()))
            lines = lax.dot_general(high, onehot[...], dims, preferred_element_type=F32)
            lines = lines + lax.dot_general(low, onehot[...], dims, preferred_element_type=F32)
            z_at = lax.broadcasted_iota(jnp.int32, (size_z, SLOTS), 0) == (cells[...] & 127)
            v = jnp.sum(jnp.where(z_at, lines, 0.0), axis=0, keepdims=True)
            values[step, cfd, c : c + 1, :] = jnp.where(live, v, 0.0)

    def z_copy(buf, block, send, recv, far, source):
        return pltpu.make_async_remote_copy(
            src_ref=buf.at[block],
            dst_ref=buf.at[block],
            send_sem=send.at[far],
            recv_sem=recv.at[source],
            device_id=(along_z(far), obs),
            device_id_type=MESH,
        )

    def z_start(buf, send, recv):
        @pl.loop(0, n_z - 1)
        def _(k):
            far = 1 + lax.rem(k + n_z // 2 - 1, n_z - 1)
            z_copy(buf, cfd, send, recv, far, far).start()

    def z_wait(buf, send, recv):
        @pl.loop(1, n_z)
        def _(far):
            source = here_y * n_z + lax.rem(here_z + n_z - far, n_z)
            z_copy(buf, source, send, recv, far, far).wait_recv()

    def z_wait_send(buf, send, recv):
        @pl.loop(1, n_z)
        def _(far):
            z_copy(buf, cfd, send, recv, far, far).wait_send()

    def y_group(buf, group, send, recv, far):
        block = pl.ds(pl.multiple_of(group * n_z, n_z), n_z)
        return pltpu.make_async_remote_copy(
            src_ref=buf.at[block],
            dst_ref=buf.at[block],
            send_sem=send.at[far],
            recv_sem=recv.at[far],
            device_id=(along_y(far), obs),
            device_id_type=MESH,
        )

    def group_at(back):
        return lax.rem(here_y + n_y - back, n_y)

    def y_start(buf, send, recv):
        for far in range(1, n_y):
            y_group(buf, here_y, send, recv, far).start()

    def y_wait_recv(buf, send, recv, far):
        y_group(buf, group_at(far), send, recv, far).wait_recv()

    def y_wait_send(buf, send, recv):
        for far in range(1, n_y):
            y_group(buf, here_y, send, recv, far).wait_send()

    def prepare(group):
        at = lax.broadcasted_iota(jnp.int32, (16, SLOTS), 0).astype(F32)
        none = jnp.zeros((16, SLOTS), BF16)

        @pl.loop(0, n_z, unroll=4)
        def _(k):
            block = group * n_z + k
            rows = meta[block]
            where = rows[0:1]
            slab = jnp.floor(where * (1.0 / (size_y * size_z)))
            inner = where - float(size_y * size_z) * slab
            line = jnp.floor(inner * (1.0 / size_z))
            place = [
                slab + ((block * size_x).astype(F32) + 0.5),
                line + ((obs * size_y).astype(F32) + 0.5),
                inner - float(size_z) * line + 0.5,
            ]
            delay = rows[1:2]
            frac = rows[2:3] * 0.25
            weights = [
                -frac * (frac - 1.0) * (frac - 2.0) / 6.0,
                (frac + 1.0) * (frac - 1.0) * (frac - 2.0) * 0.5,
                -(frac + 1.0) * frac * (frac - 2.0) * 0.5,
                (frac + 1.0) * frac * (frac - 1.0) / 6.0,
            ]
            high = jnp.floor(delay * 0.0625)
            low = delay - 16.0 * high
            first, second = jnp.zeros((16, SLOTS), F32), jnp.zeros((16, SLOTS), F32)
            for tap in range(4):
                first = jnp.where(at == low + float(tap), weights[tap], first)
                second = jnp.where(at + 16.0 == low + float(tap), weights[tap], second)
            first, second = first.astype(BF16), second.astype(BF16)
            high = jnp.broadcast_to(high, (16, SLOTS)).astype(BF16)
            before = None
            for part in range(SAMPLES // 16):
                here = high == jnp.asarray(float(part), BF16)
                band = jnp.where(here, first, none)
                if before is not None:
                    band = jnp.where(before, second, band)
                bands[block, pl.ds(part * 16, 16), :] = band
                before = here
            for start in range(0, TARGETS, 32):
                part = pl.ds(start, 32)
                d = [towards[a, part, :] - place[a] for a in range(3)]
                inv = lax.rsqrt(d[0] * d[0] + d[1] * d[1] + d[2] * d[2] + 16.0)
                four = 4.0 * inv
                square = four * inv
                greens[block, 0, part, :] = four
                for a in range(3):
                    greens[block, a + 1, part, :] = square * d[a]

    def radiate(group, steps, fresh):
        start = group * n_z
        columns = []
        for j in range(n_z):
            block = start + j
            v = [values[step, block] for step in steps]
            pieces = [[] for _ in steps]
            for begin in range(0, TARGETS, 32):
                green = [greens[block, c, pl.ds(begin, 32), :] for c in range(4)]
                for at in range(len(steps)):
                    term = green[0] * v[at][0:1]
                    for c in range(1, 4):
                        term = term + green[c] * v[at][c : c + 1]
                    pieces[at].append(term.astype(BF16))
            columns.append(jnp.concatenate([piece for step in pieces for piece in step], axis=0))
        rhs = jnp.concatenate(columns, axis=1)
        lhs = jnp.concatenate([bands[start + j] for j in range(n_z)], axis=1)
        span = slice(steps[0] * TARGETS, (steps[-1] + 1) * TARGETS)
        out = lax.dot_general(lhs, rhs, (((1,), (1,)), ((), ())), preferred_element_type=F32)
        if fresh:
            sums[:, span] = out
        else:
            sums[:, span] += out

    def meta_refs():
        return (meta, meta_z_send, meta_z_recv)

    def meta_y_refs():
        return (meta, meta_y_send, meta_y_recv)

    def val_refs(step):
        return (values.at[step], val_z_send.at[step], val_z_recv.at[step])

    def val_y_refs(step):
        return (values.at[step], val_y_send.at[step], val_y_recv.at[step])

    result_copy = pltpu.make_async_copy(last, flow_out, in_sem.at[len(inputs)])
    halos = halo_copies()
    for copy in halos:
        copy.start()
    z_start(*meta_refs())
    onehot[...] = jnp.where(
        lax.broadcasted_iota(jnp.int32, (size_x * size_y, SLOTS), 0) == row_of, 1.0, 0.0
    ).astype(BF16)
    extent = (size_x * n_cfd, size_y * n_obs, size_z)
    for a in range(3):
        line = spots[a : a + 1] * float(extent[a])
        towards[a] = jnp.transpose(jnp.broadcast_to(line, (SLOTS, TARGETS)))
    z_wait(*meta_refs())
    y_start(*meta_y_refs())
    prepare(here_y)
    for copy in halos:
        copy.wait()
    outside(0)
    for step in range(STEPS):
        advance(step)
        if step < STEPS - 1:
            outside(step + 1)
        sample(step)
        z_start(*val_refs(step))
    result_copy.start()
    for far in range(1, n_y):
        y_wait_recv(*meta_y_refs(), far)
        prepare(group_at(far))
    for step in range(STEPS):
        z_wait(*val_refs(step))
        y_start(*val_y_refs(step))
    radiate(here_y, range(STEPS), True)
    for steps in ((0, 1), (2, 3)):
        for far in range(1, n_y):
            for step in steps:
                y_wait_recv(*val_y_refs(step), far)
            radiate(group_at(far), steps, False)

    total = sums[:, :TARGETS]
    for step in range(1, STEPS):
        total = total + pltpu.roll(sums[:, step * TARGETS : (step + 1) * TARGETS], step, 0)
    whole[...] = jnp.transpose(total)

    def part_copy(far):
        return pltpu.make_async_remote_copy(
            src_ref=whole.at[pl.ds(pl.multiple_of(along_obs(far) * owned, owned), owned)],
            dst_ref=parts.at[far - 1],
            send_sem=part_send.at[far - 1],
            recv_sem=part_recv.at[far - 1],
            device_id=(cfd, along_obs(far)),
            device_id_type=MESH,
        )

    for far in range(1, n_obs):
        part_copy(far).start()
    z_wait_send(*meta_refs())
    y_wait_send(*meta_y_refs())
    for step in range(STEPS):
        z_wait_send(*val_refs(step))
        y_wait_send(*val_y_refs(step))
    result_copy.wait()
    result = whole[pl.ds(pl.multiple_of(obs * owned, owned), owned), :]
    for far in range(1, n_obs):
        part_copy(far).wait()
        result = result + parts[far - 1]
    signal[...] = result


def per_device(rings, flow_field, disk_mask, surf_cell, delay_bin, tap_phase, panel_counts, observer_pos):
    n_y, n_z, n_obs = rings
    n_cfd = n_y * n_z
    _, size_x, size_y, size_z = flow_field.shape
    wide = (size_x + 2 * WIDTH, size_y + 2 * SIDE, size_z)
    owned = TARGETS // n_obs
    dma = pltpu.SemaphoreType.DMA
    anywhere = pl.BlockSpec(memory_space=pl.ANY)
    vmem = pl.BlockSpec(memory_space=pltpu.VMEM)
    return pl.pallas_call(
        functools.partial(kernel, rings),
        out_shape=(
            jax.ShapeDtypeStruct(flow_field.shape, F32),
            jax.ShapeDtypeStruct((owned, SAMPLES), F32),
        ),
        in_specs=[anywhere] * 7,
        out_specs=(anywhere, vmem),
        scratch_shapes=[
            pltpu.VMEM(disk_mask.shape, jnp.int32),
            pltpu.VMEM(surf_cell.shape, jnp.int32),
            pltpu.VMEM(delay_bin.shape, jnp.int32),
            pltpu.VMEM(tap_phase.shape, jnp.int32),
            pltpu.VMEM(panel_counts.shape, jnp.int32),
            pltpu.VMEM(observer_pos.shape, F32),
            dma((8,)),
            pltpu.VMEM((5,) + wide, F32),
            pltpu.VMEM((STEPS - 1, 4) + wide, F32),
            pltpu.VMEM(flow_field.shape, F32),
            pltpu.VMEM((n_cfd, 4, SLOTS), F32),
            pltpu.VMEM((STEPS, n_cfd, 4, SLOTS), F32),
            pltpu.VMEM((size_x * size_y, SLOTS), BF16),
            pltpu.VMEM((3, TARGETS, SLOTS), F32),
            pltpu.VMEM((n_cfd, 4, TARGETS, SLOTS), F32),
            pltpu.VMEM((n_cfd, SAMPLES, SLOTS), BF16),
            pltpu.VMEM((SAMPLES, STEPS * TARGETS), F32),
            pltpu.VMEM((TARGETS, SAMPLES), F32),
            pltpu.VMEM((n_obs - 1, owned, SAMPLES), F32),
            dma((8,)),
            dma((8,)),
            dma((n_z,)),
            dma((n_z,)),
            dma((n_y,)),
            dma((n_y,)),
            dma((STEPS, n_z)),
            dma((STEPS, n_z)),
            dma((STEPS, n_y)),
            dma((STEPS, n_y)),
            dma((n_obs - 1,)),
            dma((n_obs - 1,)),
        ],
        compiler_params=pltpu.CompilerParams(
            collective_id=0, has_side_effects=True, vmem_limit_bytes=64 * 1024 * 1024
        ),
    )(flow_field, disk_mask, surf_cell, delay_bin, tap_phase, panel_counts, observer_pos)


def solution(mesh):
    n_cfd, n_obs = mesh.shape["cfd"], mesh.shape["obs"]
    n_y = 4 if n_cfd >= 16 else 2
    rings = (n_y, n_cfd // n_y, n_obs)
    return jax.shard_map(
        functools.partial(per_device, rings),
        mesh=mesh,
        in_specs=(
            P(None, "cfd", "obs", None),
            P("cfd", "obs", None),
            P("obs", "cfd"),
            P("obs", "cfd"),
            P("obs", "cfd"),
            P(),
            P(None, "cfd"),
        ),
        out_specs=(P(None, "cfd", "obs", None), P(("cfd", "obs"), None)),
        check_vma=False,
    )
```

time: 72.8 us -> 63.9 us (0.88)
  Pallas kernels: 65.2 us -> 60.6 us
  local copies, waits for them, and re-layouts: 6.68 us -> 2.49 us
    pallas_call x1, Pallas kernels: 65.2 us -> 60.6 us  [per_device(): pl.pallas_call(functools.partial(kernel, rings), out_shape=(jax.ShapeDtyp...]
    unnamed x16 -> x4, local copies, waits for them, and re-layouts: 6.68 us -> 2.49 us
where the time goes in v2:
time: 63.9 us; the launch traced here: 63.7 us
  Pallas kernels  60.6 us (95%)
  local copies, waits for them, and re-layouts  2.49 us (4%)
  between operations  0.65 us (1%)
    pallas_call x1, Pallas kernels, per_device(): pl.pallas_call(functools.partial(kernel, rings), out_shape=(jax.ShapeDtyp...  60.6 us
    unnamed x4, local copies, waits for them, and re-layouts  2.49 us

profile of v2, /device:TPU:1, one launch (start us, length us, event | category | flops | bytes accessed | tf_op | source)
XLA Modules:
  0.0 63.7 jit_solution(463766575988446233)
XLA Ops:
  0.6 60.6 %shard_map.86 = (f32[4,16,16,128]{3,2,1,0:T(8,128)}, f32[16,512]{1,0:T(8,128)}) custom-call(f32[4,16,16,128]{3,2,1,0:T(8,128)} %flow_in.1, s32[16,16,128]{2,1,0:T(8,128)} %disk_in.1, s32[1,128]{1,0:T(1,128)} %cells_in.1, s32[1,128]{1,0:T(1,128)} %delays_in.1, s32[1,128]{1,0:T(1,128)} %phases_in.1, s32[8,64]{1,0:T(8,128)} %counts_in.1, f32[3,128]{1,0:T(4,128)} %spots_in.1), custom_call_target="tpu_custom_call" | custom-call | tf_op jit(solution)/shard_map/pallas_call | solution.py:451
  61.2 0.0 copy-start
  61.2 1.9 %copy.11 = f32[4,16,16,128]{3,2,1,0:T(8,128)} copy(f32[4,16,16,128]{3,2,1,0:T(8,128)} %get-tuple-element.4) | data formatting | bytes 1048576
  63.1 0.0 copy-done
  63.1 0.6 copy.12
Async XLA Ops:
  61.2 1.9 %copy-start = (f32[16,512]{1,0:T(8,128)S(1)}, f32[16,512]{1,0:T(8,128)}, u32[]{:S(2)}) copy-start(f32[16,512]{1,0:T(8,128)} %get-tuple-element.5) | copy-start | bytes 98308

commit v3 on v2

--- a/solution.py
+++ b/solution.py
@@ -37,6 +37,10 @@
     spots,
     in_sem,
     wide,
+    y_send,
+    y_recv,
+    corner_send,
+    corner_recv,
     state,
     last,
     meta,
@@ -139,35 +143,62 @@
         ],
         axis=0,
     )
-    pl.semaphore_wait(barrier, 6 + n_z - 1 + n_y - 1 + n_obs - 1)
+
+    last_x, last_y = WIDTH + size_x - 1, SIDE + size_y - 1
+    corners = [
+        (x_side, y_side)
+        for x_side in ((cfd_next, last_x, -1, WIDTH - 1), (cfd_prev, WIDTH, 1, last_x + 1))
+        for y_side in ((obs_next, True), (obs_prev, False))
+    ]
+
+    def pack():
+        y_send[0] = wide[:, own_x, last_y - WIDTH + 1 : last_y + 1]
+        y_send[1] = wide[:, own_x, SIDE : SIDE + WIDTH]
+        for at, ((_, x, turn, _), (_, upper)) in enumerate(corners):
+            for c in range(5):
+                pieces = []
+                for far in range(1, WIDTH):
+                    many = WIDTH - far
+                    rows = slice(last_y + 1 - many, last_y + 1) if upper else slice(SIDE, SIDE + many)
+                    pieces.append(wide[c, x + turn * (far - 1), rows])
+                corner_send[at, c] = jnp.concatenate(pieces + [jnp.zeros((2, size_z), F32)], axis=0)
+
+    def unpack():
+        wide[:, own_x, SIDE - WIDTH : SIDE] = y_recv[0]
+        wide[:, own_x, last_y + 1 : last_y + 1 + WIDTH] = y_recv[1]
+        for at, ((_, _, turn, x), (_, upper)) in enumerate(corners):
+            for c in range(5):
+                begin = 0
+                for far in range(1, WIDTH):
+                    many = WIDTH - far
+                    rows = slice(SIDE - many, SIDE) if upper else slice(last_y + 1, last_y + 1 + many)
+                    wide[c, x + turn * (far - 1), rows] = corner_recv[at, c, begin : begin + many]
+                    begin += many
 
     def halo_copies():
-        low_x, high_x = slice(0, WIDTH), slice(WIDTH + size_x, 2 * WIDTH + size_x)
-        low_y, high_y = slice(0, SIDE), slice(SIDE + size_y, tall)
-        first_x, last_x = slice(WIDTH, 2 * WIDTH), slice(size_x, size_x + WIDTH)
-        first_y, last_y = slice(SIDE, 2 * SIDE), slice(size_y, size_y + SIDE)
-        low_c, high_c = slice(1, WIDTH), slice(WIDTH + size_x, 2 * WIDTH + size_x - 1)
-        first_c, last_c = slice(WIDTH, 2 * WIDTH - 1), slice(size_x + 1, size_x + WIDTH)
         moves = [
-            (last_x, own_y, low_x, own_y, cfd_next, obs),
-            (first_x, own_y, high_x, own_y, cfd_prev, obs),
-            (last_c, last_y, low_c, low_y, cfd_next, obs_next),
-            (last_c, first_y, low_c, high_y, cfd_next, obs_prev),
-            (first_c, last_y, high_c, low_y, cfd_prev, obs_next),
-            (first_c, first_y, high_c, high_y, cfd_prev, obs_prev),
-            (own_x, last_y, own_x, low_y, cfd, obs_next),
-            (own_x, first_y, own_x, high_y, cfd, obs_prev),
+            (wide.at[:, size_x : size_x + WIDTH, own_y], wide.at[:, 0:WIDTH, own_y], cfd_next, obs),
+            (
+                wide.at[:, WIDTH : 2 * WIDTH, own_y],
+                wide.at[:, WIDTH + size_x : 2 * WIDTH + size_x, own_y],
+                cfd_prev,
+                obs,
+            ),
+            (y_send.at[0], y_recv.at[0], cfd, obs_next),
+            (y_send.at[1], y_recv.at[1], cfd, obs_prev),
         ]
+        for at, ((to_cfd, _, _, _), (to_obs, _)) in enumerate(corners):
+            moves.append((corner_send.at[at], corner_recv.at[at], to_cfd, to_obs))
         return [
             pltpu.make_async_remote_copy(
-                src_ref=wide.at[:, from_x, from_y],
-                dst_ref=wide.at[:, to_x, to_y],
+                src_ref=source,
+                dst_ref=target,
                 send_sem=halo_send.at[i],
                 recv_sem=halo_recv.at[i],
                 device_id=(to_cfd, to_obs),
                 device_id_type=MESH,
             )
-            for i, (from_x, from_y, to_x, to_y, to_cfd, to_obs) in enumerate(moves)
+            for i, (source, target, to_cfd, to_obs) in enumerate(moves)
         ]
 
     def fields(step):
@@ -335,7 +366,7 @@
                 for a in range(3):
                     greens[block, a + 1, part, :] = square * d[a]
 
-    def radiate(group, steps, fresh):
+    def radiate(group, steps):
         start = group * n_z
         columns = []
         for j in range(n_z):
@@ -354,10 +385,7 @@
         lhs = jnp.concatenate([bands[start + j] for j in range(n_z)], axis=1)
         span = slice(steps[0] * TARGETS, (steps[-1] + 1) * TARGETS)
         out = lax.dot_general(lhs, rhs, (((1,), (1,)), ((), ())), preferred_element_type=F32)
-        if fresh:
-            sums[:, span] = out
-        else:
-            sums[:, span] += out
+        sums[:, span] += out
 
     def meta_refs():
         return (meta, meta_z_send, meta_z_recv)
@@ -371,6 +399,8 @@
     def val_y_refs(step):
         return (values.at[step], val_y_send.at[step], val_y_recv.at[step])
 
+    pack()
+    pl.semaphore_wait(barrier, 6 + n_z - 1 + n_y - 1 + n_obs - 1)
     result_copy = pltpu.make_async_copy(last, flow_out, in_sem.at[len(inputs)])
     halos = halo_copies()
     for copy in halos:
@@ -383,11 +413,9 @@
     for a in range(3):
         line = spots[a : a + 1] * float(extent[a])
         towards[a] = jnp.transpose(jnp.broadcast_to(line, (SLOTS, TARGETS)))
-    z_wait(*meta_refs())
-    y_start(*meta_y_refs())
-    prepare(here_y)
     for copy in halos:
         copy.wait()
+    unpack()
     outside(0)
     for step in range(STEPS):
         advance(step)
@@ -395,19 +423,29 @@
             outside(step + 1)
         sample(step)
         z_start(*val_refs(step))
+        if step == 0:
+            z_wait(*meta_refs())
+            y_start(*meta_y_refs())
     result_copy.start()
-    for far in range(1, n_y):
+    prepare(here_y)
+
+    @pl.loop(1, n_y)
+    def _(far):
         y_wait_recv(*meta_y_refs(), far)
         prepare(group_at(far))
+
     for step in range(STEPS):
         z_wait(*val_refs(step))
         y_start(*val_y_refs(step))
-    radiate(here_y, range(STEPS), True)
+    sums[...] = jnp.zeros_like(sums)
+    radiate(here_y, range(STEPS))
     for steps in ((0, 1), (2, 3)):
-        for far in range(1, n_y):
+
+        @pl.loop(1, n_y)
+        def _(far):
             for step in steps:
                 y_wait_recv(*val_y_refs(step), far)
-            radiate(group_at(far), steps, False)
+            radiate(group_at(far), steps)
 
     total = sums[:, :TARGETS]
     for step in range(1, STEPS):
@@ -465,6 +503,10 @@
             pltpu.VMEM(observer_pos.shape, F32),
             dma((8,)),
             pltpu.VMEM((5,) + wide, F32),
+            pltpu.VMEM((2, 5, size_x, WIDTH, size_z), F32),
+            pltpu.VMEM((2, 5, size_x, WIDTH, size_z), F32),
+            pltpu.VMEM((4, 5, 8, size_z), F32),
+            pltpu.VMEM((4, 5, 8, size_z), F32),
             pltpu.VMEM((STEPS - 1, 4) + wide, F32),
             pltpu.VMEM(flow_field.shape, F32),
             pltpu.VMEM((n_cfd, 4, SLOTS), F32),

time: 63.9 us -> 57.6 us (0.901)
  Pallas kernels: 60.6 us -> 54.3 us
    pallas_call x1, Pallas kernels: 60.6 us -> 54.3 us  [per_device(): pl.pallas_call(functools.partial(kernel, rings), out_shape=(jax.ShapeDtyp...]
where the time goes in v3:
time: 57.6 us; the launch traced here: 57.4 us
  Pallas kernels  54.3 us (94%)
  local copies, waits for them, and re-layouts  2.49 us (4%)
  between operations  0.65 us (1%)
    pallas_call x1, Pallas kernels, per_device(): pl.pallas_call(functools.partial(kernel, rings), out_shape=(jax.ShapeDtyp...  54.3 us
    unnamed x4, local copies, waits for them, and re-layouts  2.49 us

profile of v3, /device:TPU:1, one launch (start us, length us, event | category | flops | bytes accessed | tf_op | source)
XLA Modules:
  0.0 57.4 jit_solution(11258682561928044856)
XLA Ops:
  0.6 54.3 %shard_map.86 = (f32[4,16,16,128]{3,2,1,0:T(8,128)}, f32[16,512]{1,0:T(8,128)}) custom-call(f32[4,16,16,128]{3,2,1,0:T(8,128)} %flow_in.1, s32[16,16,128]{2,1,0:T(8,128)} %disk_in.1, s32[1,128]{1,0:T(1,128)} %cells_in.1, s32[1,128]{1,0:T(1,128)} %delays_in.1, s32[1,128]{1,0:T(1,128)} %phases_in.1, s32[8,64]{1,0:T(8,128)} %counts_in.1, f32[3,128]{1,0:T(4,128)} %spots_in.1), custom_call_target="tpu_custom_call" | custom-call | tf_op jit(solution)/shard_map/pallas_call | solution.py:489
  54.9 0.0 copy-start
  54.9 1.9 %copy.11 = f32[4,16,16,128]{3,2,1,0:T(8,128)} copy(f32[4,16,16,128]{3,2,1,0:T(8,128)} %get-tuple-element.4) | data formatting | bytes 1048576
  56.8 0.0 copy-done
  56.8 0.6 %copy.12 = f32[16,512]{1,0:T(8,128)} copy(f32[16,512]{1,0:T(8,128)S(1)} %copy-done) | data formatting | bytes 65536
Async XLA Ops:
  54.9 1.9 %copy-start = (f32[16,512]{1,0:T(8,128)S(1)}, f32[16,512]{1,0:T(8,128)}, u32[]{:S(2)}) copy-start(f32[16,512]{1,0:T(8,128)} %get-tuple-element.5) | copy-start | bytes 98308

commit v4 on v3

--- a/solution.py
+++ b/solution.py
@@ -163,9 +163,11 @@
                     pieces.append(wide[c, x + turn * (far - 1), rows])
                 corner_send[at, c] = jnp.concatenate(pieces + [jnp.zeros((2, size_z), F32)], axis=0)
 
-    def unpack():
+    def unpack_y():
         wide[:, own_x, SIDE - WIDTH : SIDE] = y_recv[0]
         wide[:, own_x, last_y + 1 : last_y + 1 + WIDTH] = y_recv[1]
+
+    def unpack_corners():
         for at, ((_, _, turn, x), (_, upper)) in enumerate(corners):
             for c in range(5):
                 begin = 0
@@ -177,6 +179,8 @@
 
     def halo_copies():
         moves = [
+            (y_send.at[0], y_recv.at[0], cfd, obs_next),
+            (y_send.at[1], y_recv.at[1], cfd, obs_prev),
             (wide.at[:, size_x : size_x + WIDTH, own_y], wide.at[:, 0:WIDTH, own_y], cfd_next, obs),
             (
                 wide.at[:, WIDTH : 2 * WIDTH, own_y],
@@ -184,8 +188,6 @@
                 cfd_prev,
                 obs,
             ),
-            (y_send.at[0], y_recv.at[0], cfd, obs_next),
-            (y_send.at[1], y_recv.at[1], cfd, obs_prev),
         ]
         for at, ((to_cfd, _, _, _), (to_obs, _)) in enumerate(corners):
             moves.append((corner_send.at[at], corner_recv.at[at], to_cfd, to_obs))
@@ -204,7 +206,7 @@
     def fields(step):
         return wide if step == 0 else state.at[step - 1]
 
-    def outside(step):
+    def outside_x(step):
         ref = fields(step)
 
         @pl.when(cfd == 0)
@@ -215,6 +217,9 @@
         def _():
             ref[0:4, WIDTH + size_x :] = jnp.zeros((4, WIDTH, tall, size_z), F32)
 
+    def outside_y(step):
+        ref = fields(step)
+
         @pl.when(obs == 0)
         def _():
             ref[0:4, :, 0:SIDE] = jnp.zeros((4, size_x + 2 * WIDTH, SIDE, size_z), F32)
@@ -225,11 +230,11 @@
 
     lane = lax.broadcasted_iota(jnp.int32, (tall, size_z), 1)
 
-    def advance(step):
+    def advance(step, begin, end):
         ref = fields(step)
         final = step == STEPS - 1
 
-        @pl.loop(1 + step, 2 * WIDTH + size_x - 1 - step, unroll=True)
+        @pl.loop(begin, end, unroll=True)
         def _(i):
             slabs = [ref[c, i] for c in range(4)]
             there = wide[4, i]
@@ -261,7 +266,8 @@
             lines = lines + lax.dot_general(low, onehot[...], dims, preferred_element_type=F32)
             z_at = lax.broadcasted_iota(jnp.int32, (size_z, SLOTS), 0) == (cells[...] & 127)
             v = jnp.sum(jnp.where(z_at, lines, 0.0), axis=0, keepdims=True)
-            values[step, cfd, c : c + 1, :] = jnp.where(live, v, 0.0)
+            at = step % 2 * 4 + c
+            values[step // 2, cfd, at : at + 1, :] = jnp.where(live, v, 0.0)
 
     def z_copy(buf, block, send, recv, far, source):
         return pltpu.make_async_remote_copy(
@@ -276,7 +282,7 @@
     def z_start(buf, send, recv):
         @pl.loop(0, n_z - 1)
         def _(k):
-            far = 1 + lax.rem(k + n_z // 2 - 1, n_z - 1)
+            far = n_z // 2 + (1 - 2 * (k % 2)) * ((k + 1) // 2)
             z_copy(buf, cfd, send, recv, far, far).start()
 
     def z_wait(buf, send, recv):
@@ -371,7 +377,7 @@
         columns = []
         for j in range(n_z):
             block = start + j
-            v = [values[step, block] for step in steps]
+            v = [values[step // 2, block, step % 2 * 4 : step % 2 * 4 + 4] for step in steps]
             pieces = [[] for _ in steps]
             for begin in range(0, TARGETS, 32):
                 green = [greens[block, c, pl.ds(begin, 32), :] for c in range(4)]
@@ -393,11 +399,11 @@
     def meta_y_refs():
         return (meta, meta_y_send, meta_y_recv)
 
-    def val_refs(step):
-        return (values.at[step], val_z_send.at[step], val_z_recv.at[step])
-
-    def val_y_refs(step):
-        return (values.at[step], val_y_send.at[step], val_y_recv.at[step])
+    def val_refs(half):
+        return (values.at[half], val_z_send.at[half], val_z_recv.at[half])
+
+    def val_y_refs(half):
+        return (values.at[half], val_y_send.at[half], val_y_recv.at[half])
 
     pack()
     pl.semaphore_wait(barrier, 6 + n_z - 1 + n_y - 1 + n_obs - 1)
@@ -413,39 +419,56 @@
     for a in range(3):
         line = spots[a : a + 1] * float(extent[a])
         towards[a] = jnp.transpose(jnp.broadcast_to(line, (SLOTS, TARGETS)))
-    for copy in halos:
+    for copy in halos[:2]:
         copy.wait()
-    unpack()
-    outside(0)
+    unpack_y()
+    outside_y(0)
     for step in range(STEPS):
-        advance(step)
+        advance(step, WIDTH + 1 + step, WIDTH + size_x - 1 - step)
         if step < STEPS - 1:
-            outside(step + 1)
-        sample(step)
-        z_start(*val_refs(step))
-        if step == 0:
+            outside_y(step + 1)
+    for copy in halos[2:]:
+        copy.wait()
+    unpack_corners()
+    outside_x(0)
+    outside_y(0)
+    for step in range(STEPS):
+        advance(step, 1 + step, WIDTH + 1 + step)
+        advance(step, WIDTH + size_x - 1 - step, 2 * WIDTH + size_x - 1 - step)
+        if step < STEPS - 1:
+            outside_x(step + 1)
+            outside_y(step + 1)
+        if step % 2 == 1:
+            sample(step - 1)
+            sample(step)
+            z_start(*val_refs(step // 2))
+        if step == 1:
             z_wait(*meta_refs())
             y_start(*meta_y_refs())
     result_copy.start()
     prepare(here_y)
 
+    def arrival(k):
+        return 1 + 2 * (k - 1) % (n_y - 1)
+
     @pl.loop(1, n_y)
-    def _(far):
+    def _(k):
+        far = arrival(k)
         y_wait_recv(*meta_y_refs(), far)
         prepare(group_at(far))
 
-    for step in range(STEPS):
-        z_wait(*val_refs(step))
-        y_start(*val_y_refs(step))
+    for half in range(2):
+        z_wait(*val_refs(half))
+        y_start(*val_y_refs(half))
     sums[...] = jnp.zeros_like(sums)
     radiate(here_y, range(STEPS))
-    for steps in ((0, 1), (2, 3)):
+    for half in range(2):
 
         @pl.loop(1, n_y)
-        def _(far):
-            for step in steps:
-                y_wait_recv(*val_y_refs(step), far)
-            radiate(group_at(far), steps)
+        def _(k):
+            far = arrival(k)
+            y_wait_recv(*val_y_refs(half), far)
+            radiate(group_at(far), (2 * half, 2 * half + 1))
 
     total = sums[:, :TARGETS]
     for step in range(1, STEPS):
@@ -462,13 +485,13 @@
             device_id_type=MESH,
         )
 
-    for far in range(1, n_obs):
+    for far in sorted(range(1, n_obs), key=lambda far: abs(far - n_obs // 2)):
         part_copy(far).start()
     z_wait_send(*meta_refs())
     y_wait_send(*meta_y_refs())
-    for step in range(STEPS):
-        z_wait_send(*val_refs(step))
-        y_wait_send(*val_y_refs(step))
+    for half in range(2):
+        z_wait_send(*val_refs(half))
+        y_wait_send(*val_y_refs(half))
     result_copy.wait()
     result = whole[pl.ds(pl.multiple_of(obs * owned, owned), owned), :]
     for far in range(1, n_obs):
@@ -510,7 +533,7 @@
             pltpu.VMEM((STEPS - 1, 4) + wide, F32),
             pltpu.VMEM(flow_field.shape, F32),
             pltpu.VMEM((n_cfd, 4, SLOTS), F32),
-            pltpu.VMEM((STEPS, n_cfd, 4, SLOTS), F32),
+            pltpu.VMEM((STEPS // 2, n_cfd, 8, SLOTS), F32),
             pltpu.VMEM((size_x * size_y, SLOTS), BF16),
             pltpu.VMEM((3, TARGETS, SLOTS), F32),
             pltpu.VMEM((n_cfd, 4, TARGETS, SLOTS), F32),
@@ -524,10 +547,10 @@
             dma((n_z,)),
             dma((n_y,)),
             dma((n_y,)),
-            dma((STEPS, n_z)),
-            dma((STEPS, n_z)),
-            dma((STEPS, n_y)),
-            dma((STEPS, n_y)),
+            dma((STEPS // 2, n_z)),
+            dma((STEPS // 2, n_z)),
+            dma((STEPS // 2, n_y)),
+            dma((STEPS // 2, n_y)),
             dma((n_obs - 1,)),
             dma((n_obs - 1,)),
         ],

time: 57.6 us -> 53.8 us (0.934)
  Pallas kernels: 54.3 us -> 50.5 us
    pallas_call x1, Pallas kernels: 54.3 us -> 50.5 us  [per_device(): pl.pallas_call(functools.partial(kernel, rings), out_shape=(jax.ShapeDtyp...]
where the time goes in v4:
time: 53.8 us; the launch traced here: 53.6 us
  Pallas kernels  50.5 us (94%)
  local copies, waits for them, and re-layouts  2.49 us (5%)
  between operations  0.65 us (1%)
    pallas_call x1, Pallas kernels, per_device(): pl.pallas_call(functools.partial(kernel, rings), out_shape=(jax.ShapeDtyp...  50.5 us
    unnamed x4, local copies, waits for them, and re-layouts  2.49 us

profile of v4, /device:TPU:1, one launch (start us, length us, event | category | flops | bytes accessed | tf_op | source)
XLA Modules:
  0.0 53.6 jit_solution(4698893192427360861)
XLA Ops:
  0.6 50.5 %shard_map.86 = (f32[4,16,16,128]{3,2,1,0:T(8,128)}, f32[16,512]{1,0:T(8,128)}) custom-call(f32[4,16,16,128]{3,2,1,0:T(8,128)} %flow_in.1, s32[16,16,128]{2,1,0:T(8,128)} %disk_in.1, s32[1,128]{1,0:T(1,128)} %cells_in.1, s32[1,128]{1,0:T(1,128)} %delays_in.1, s32[1,128]{1,0:T(1,128)} %phases_in.1, s32[8,64]{1,0:T(8,128)} %counts_in.1, f32[3,128]{1,0:T(4,128)} %spots_in.1), custom_call_target="tpu_custom_call" | custom-call | tf_op jit(solution)/shard_map/pallas_call | solution.py:512
  51.1 0.0 copy-start
  51.1 1.9 %copy.11 = f32[4,16,16,128]{3,2,1,0:T(8,128)} copy(f32[4,16,16,128]{3,2,1,0:T(8,128)} %get-tuple-element.4) | data formatting | bytes 1048576
  53.0 0.0 copy-done
  53.0 0.6 %copy.12 = f32[16,512]{1,0:T(8,128)} copy(f32[16,512]{1,0:T(8,128)S(1)} %copy-done) | data formatting | bytes 65536
Async XLA Ops:
  51.1 1.9 %copy-start = (f32[16,512]{1,0:T(8,128)S(1)}, f32[16,512]{1,0:T(8,128)}, u32[]{:S(2)}) copy-start(f32[16,512]{1,0:T(8,128)} %get-tuple-element.5) | copy-start | bytes 98308

commit v5 on v4

--- a/solution.py
+++ b/solution.py
@@ -89,6 +89,21 @@
     cfd_next, cfd_prev = lax.rem(cfd + 1, n_cfd), lax.rem(cfd + n_cfd - 1, n_cfd)
     obs_next, obs_prev = along_obs(1), along_obs(n_obs - 1)
 
+    barrier = pltpu.get_barrier_semaphore()
+
+    def greet(to_cfd, to_obs):
+        pl.semaphore_signal(barrier, inc=1, device_id=(to_cfd, to_obs), device_id_type=MESH)
+
+    for far in sorted(range(1, n_z), key=lambda far: abs(far - n_z // 2)):
+        greet(along_z(far), obs)
+    for to_cfd in (cfd_next, cfd_prev):
+        for to_obs in (obs_next, obs_prev, obs):
+            greet(to_cfd, to_obs)
+    for far in range(1, n_y):
+        greet(along_y(far), obs)
+    for far in range(1, n_obs):
+        greet(cfd, along_obs(far))
+
     inputs = [
         pltpu.make_async_copy(src, dst, in_sem.at[i])
         for i, (src, dst) in enumerate(
@@ -105,21 +120,6 @@
     ]
     for copy in inputs:
         copy.start()
-
-    barrier = pltpu.get_barrier_semaphore()
-
-    def greet(to_cfd, to_obs):
-        pl.semaphore_signal(barrier, inc=1, device_id=(to_cfd, to_obs), device_id_type=MESH)
-
-    for to_cfd in (cfd_next, cfd_prev):
-        for to_obs in (obs_next, obs_prev, obs):
-            greet(to_cfd, to_obs)
-    for far in range(1, n_z):
-        greet(along_z(far), obs)
-    for far in range(1, n_y):
-        greet(along_y(far), obs)
-    for far in range(1, n_obs):
-        greet(cfd, along_obs(far))
 
     inputs[0].wait()
     for i in range(size_x):
@@ -280,19 +280,19 @@
         )
 
     def z_start(buf, send, recv):
-        @pl.loop(0, n_z - 1)
+        @pl.loop(0, n_z - 1, unroll=True)
         def _(k):
             far = n_z // 2 + (1 - 2 * (k % 2)) * ((k + 1) // 2)
             z_copy(buf, cfd, send, recv, far, far).start()
 
     def z_wait(buf, send, recv):
-        @pl.loop(1, n_z)
+        @pl.loop(1, n_z, unroll=True)
         def _(far):
             source = here_y * n_z + lax.rem(here_z + n_z - far, n_z)
             z_copy(buf, source, send, recv, far, far).wait_recv()
 
     def z_wait_send(buf, send, recv):
-        @pl.loop(1, n_z)
+        @pl.loop(1, n_z, unroll=True)
         def _(far):
             z_copy(buf, cfd, send, recv, far, far).wait_send()
 
@@ -409,7 +409,7 @@
     pl.semaphore_wait(barrier, 6 + n_z - 1 + n_y - 1 + n_obs - 1)
     result_copy = pltpu.make_async_copy(last, flow_out, in_sem.at[len(inputs)])
     halos = halo_copies()
-    for copy in halos:
+    for copy in halos[2:] + halos[:2]:
         copy.start()
     z_start(*meta_refs())
     onehot[...] = jnp.where(

time: 53.8 us -> 53.5 us (level)
  no operation moved by 1% of the time
where the time goes in v5:
time: 53.5 us; the launch traced here: 53.3 us
  Pallas kernels  50.2 us (94%)
  local copies, waits for them, and re-layouts  2.49 us (5%)
  between operations  0.65 us (1%)
    pallas_call x1, Pallas kernels, per_device(): pl.pallas_call(functools.partial(kernel, rings), out_shape=(jax.ShapeDtyp...  50.2 us
    unnamed x4, local copies, waits for them, and re-layouts  2.49 us

profile of v5, /device:TPU:1, one launch (start us, length us, event | category | flops | bytes accessed | tf_op | source)
XLA Modules:
  0.0 53.3 jit_solution(3170732530514387615)
XLA Ops:
  0.6 50.2 %shard_map.86 = (f32[4,16,16,128]{3,2,1,0:T(8,128)}, f32[16,512]{1,0:T(8,128)}) custom-call(f32[4,16,16,128]{3,2,1,0:T(8,128)} %flow_in.1, s32[16,16,128]{2,1,0:T(8,128)} %disk_in.1, s32[1,128]{1,0:T(1,128)} %cells_in.1, s32[1,128]{1,0:T(1,128)} %delays_in.1, s32[1,128]{1,0:T(1,128)} %phases_in.1, s32[8,64]{1,0:T(8,128)} %counts_in.1, f32[3,128]{1,0:T(4,128)} %spots_in.1), custom_call_target="tpu_custom_call" | custom-call | tf_op jit(solution)/shard_map/pallas_call | solution.py:512
  50.8 0.0 copy-start
  50.8 1.9 %copy.11 = f32[4,16,16,128]{3,2,1,0:T(8,128)} copy(f32[4,16,16,128]{3,2,1,0:T(8,128)} %get-tuple-element.4) | data formatting | bytes 1048576
  52.7 0.0 copy-done
  52.7 0.6 %copy.12 = f32[16,512]{1,0:T(8,128)} copy(f32[16,512]{1,0:T(8,128)S(1)} %copy-done) | data formatting | bytes 65536
Async XLA Ops:
  50.8 1.9 %copy-start = (f32[16,512]{1,0:T(8,128)S(1)}, f32[16,512]{1,0:T(8,128)}, u32[]{:S(2)}) copy-start(f32[16,512]{1,0:T(8,128)} %get-tuple-element.5) | copy-start | bytes 98308

commit v6 on v5

--- a/solution.py
+++ b/solution.py
@@ -368,9 +368,9 @@
                 inv = lax.rsqrt(d[0] * d[0] + d[1] * d[1] + d[2] * d[2] + 16.0)
                 four = 4.0 * inv
                 square = four * inv
-                greens[block, 0, part, :] = four
+                greens[block, 0, part, :] = four.astype(BF16).astype(F32)
                 for a in range(3):
-                    greens[block, a + 1, part, :] = square * d[a]
+                    greens[block, a + 1, part, :] = (square * d[a]).astype(BF16).astype(F32)
 
     def radiate(group, steps):
         start = group * n_z

time: 53.5 us -> 54 us (level)
    pallas_call x1, Pallas kernels: 50.2 us -> 50.7 us  [per_device(): pl.pallas_call(functools.partial(kernel, rings), out_shape=(jax.ShapeDtyp...]
where the time goes in v6:
time: 54 us; the launch traced here: 53.9 us
  Pallas kernels  50.7 us (94%)
  local copies, waits for them, and re-layouts  2.49 us (5%)
  between operations  0.65 us (1%)
    pallas_call x1, Pallas kernels, per_device(): pl.pallas_call(functools.partial(kernel, rings), out_shape=(jax.ShapeDtyp...  50.7 us
    unnamed x4, local copies, waits for them, and re-layouts  2.49 us

profile of v6, /device:TPU:1, one launch (start us, length us, event | category | flops | bytes accessed | tf_op | source)
XLA Modules:
  0.0 53.9 jit_solution(481004233779016272)
XLA Ops:
  0.6 50.7 %shard_map.86 = (f32[4,16,16,128]{3,2,1,0:T(8,128)}, f32[16,512]{1,0:T(8,128)}) custom-call(f32[4,16,16,128]{3,2,1,0:T(8,128)} %flow_in.1, s32[16,16,128]{2,1,0:T(8,128)} %disk_in.1, s32[1,128]{1,0:T(1,128)} %cells_in.1, s32[1,128]{1,0:T(1,128)} %delays_in.1, s32[1,128]{1,0:T(1,128)} %phases_in.1, s32[8,64]{1,0:T(8,128)} %counts_in.1, f32[3,128]{1,0:T(4,128)} %spots_in.1), custom_call_target="tpu_custom_call" | custom-call | tf_op jit(solution)/shard_map/pallas_call | solution.py:512
  51.4 0.0 copy-start
  51.4 1.9 %copy.11 = f32[4,16,16,128]{3,2,1,0:T(8,128)} copy(f32[4,16,16,128]{3,2,1,0:T(8,128)} %get-tuple-element.4) | data formatting | bytes 1048576
  53.3 0.0 copy-done
  53.3 0.6 %copy.12 = f32[16,512]{1,0:T(8,128)} copy(f32[16,512]{1,0:T(8,128)S(1)} %copy-done) | data formatting | bytes 65536
Async XLA Ops:
  51.4 1.9 %copy-start = (f32[16,512]{1,0:T(8,128)S(1)}, f32[16,512]{1,0:T(8,128)}, u32[]{:S(2)}) copy-start(f32[16,512]{1,0:T(8,128)} %get-tuple-element.5) | copy-start | bytes 98308
